TPU v7x, 256 devices: a whole 4x4x8 slice. The times are simulated.
256 devices in a mesh: dp: 64 (over x, z, y_hi), mp: 4 (over y_lo, core).
Axes of the slice: x: 4, y: 4 (y_hi: 2, y_lo: 2; y = y_hi * 2 + y_lo), z: 8, core: 2. Of those that a mesh axis runs over, the one named last changes fastest.
Arguments:
- patches: bfloat16 [131072, 1152], P('dp', 'mp')
- counts: int32 [128], P('dp'), may hold values from 256 to 1024, as said below
- pair_ids: int32 [128], P('dp'), may hold values from 0 to 127, each once
- inner_weight: bfloat16 [1152, 4304], P(None, 'mp'), may hold values from -0.1875 to 0.1875
- outer_weight: bfloat16 [4304, 1152], P('mp'), may hold values from -0.09375 to 0.09375
- text_embed: bfloat16 [128, 1152], P('dp', 'mp')
- log_scale: float32 [1], replicated, may hold values from 1.5 to 2.5
- logit_bias: float32 [1], replicated, may hold values from -5 to -2
Outputs:
- image_loss: float32 [128], P('dp')
- emb_grad: float32 [128, 1152], P('dp', 'mp')
- text_grad: float32 [128, 1152], P('dp', 'mp')
Inputs may be any that keep to these rules, and one draw needn't show every extreme that they name: `counts`: in every draw the images of some shard fill all of its 2048 rows. `pair_ids`: each text index appears once.
All inputs are finite; a program needn't handle non-finite values.
Results may differ from a plain program's by a relative error of at most 0.0036.
Values may be sent and summed in bfloat16 or wider, within the bound.
A program may use at most 128 MiB of HBM per device.

v0:
```python
import jax
import jax.numpy as jnp
from jax import lax
from jax.sharding import PartitionSpec as P

epsilon = 1e-06


def layer_norm(values):
    centre = jnp.mean(values, axis=-1, keepdims=True)
    shifted = values - centre
    spread = jnp.mean(shifted * shifted, axis=-1, keepdims=True)
    return shifted * lax.rsqrt(spread + epsilon)


def expand_rows(normed, weights):
    return jax.nn.gelu(
        jnp.dot(normed, weights, preferred_element_type=jnp.float32), approximate=True
    )


def shards(
    patches, counts, pair_ids, inner_weight, outer_weight, text_embed, log_scale, logit_bias
):
    group_size = lax.axis_size("mp")
    shard_rows = patches.shape[0]
    own_count = shard_rows // group_size
    row_first = lax.axis_index("mp") * own_count
    full_rows = lax.all_gather(patches, "mp", axis=1, tiled=True)
    normed = layer_norm(full_rows.astype(jnp.float32)).astype(jnp.bfloat16)
    hidden = expand_rows(normed, inner_weight).astype(jnp.bfloat16)
    mixed_rows = lax.psum_scatter(
        jnp.dot(hidden, outer_weight, preferred_element_type=jnp.float32),
        "mp",
        scatter_dimension=0,
        tiled=True,
    )
    own_rows = lax.dynamic_slice_in_dim(full_rows, row_first, own_count, 0)
    updated = own_rows.astype(jnp.float32) + mixed_rows
    final_rows = layer_norm(updated)
    row_ends = jnp.cumsum(counts)
    row_starts = row_ends - counts
    row_ids = row_first + jnp.arange(own_count, dtype=jnp.int32)
    member = (
        (row_ids[None, :] >= row_starts[:, None]) & (row_ids[None, :] < row_ends[:, None])
    ).astype(jnp.float32)
    partial_value = jnp.dot(member, final_rows, precision=lax.Precision.HIGHEST)
    pooled = lax.psum(partial_value, "mp") / counts[:, None].astype(jnp.float32)
    image_norm = lax.rsqrt(jnp.sum(pooled * pooled, axis=1) + epsilon)
    unit_image = pooled * image_norm[:, None]
    image_wire = unit_image.astype(jnp.bfloat16)
    image_values = image_wire.astype(jnp.float32)
    text_full = lax.all_gather(text_embed, "mp", axis=1, tiled=True)
    text_values = text_full.astype(jnp.float32)
    text_norm = lax.rsqrt(jnp.sum(text_values * text_values, axis=1) + epsilon)
    text_unit = text_values * text_norm[:, None]
    text_wire = text_unit.astype(jnp.bfloat16)
    logit_scale = jnp.exp(log_scale[0])
    offset = logit_bias[0]
    text_rows = text_wire.shape[0]
    all_text = lax.all_gather(text_wire, "dp", axis=0, tiled=True)
    logits = (
        logit_scale * jnp.dot(image_wire, all_text.T, preferred_element_type=jnp.float32) + offset
    )
    text_ids = 0 * text_rows + jnp.arange(all_text.shape[0], dtype=jnp.int32)
    labels = jnp.where(pair_ids[:, None] == text_ids[None, :], 1.0, -1.0).astype(jnp.float32)
    visit_loss_sum = jnp.sum(jax.nn.softplus(-labels * logits), axis=1)
    slopes = -labels * jax.nn.sigmoid(-labels * logits)
    visit_image_dir = jnp.dot(slopes, all_text.astype(jnp.float32), precision=lax.Precision.HIGHEST)
    text_term = jnp.dot(slopes.T, image_values, precision=lax.Precision.HIGHEST)
    image_dir, loss_sum, text_term = (visit_image_dir, visit_loss_sum, text_term)
    text_dir = lax.psum_scatter(text_term, "dp", scatter_dimension=0, tiled=True)
    image_dir = logit_scale * image_dir
    text_dir = logit_scale * text_dir
    image_proj = jnp.sum(unit_image * image_dir, axis=1, keepdims=True)
    emb_whole = (image_dir - unit_image * image_proj) * image_norm[:, None]
    text_proj = jnp.sum(text_unit * text_dir, axis=1, keepdims=True)
    text_whole = (text_dir - text_unit * text_proj) * text_norm[:, None]
    local_width = text_embed.shape[1]
    feature_first = lax.axis_index("mp") * local_width
    emb_grad = lax.dynamic_slice_in_dim(emb_whole, feature_first, local_width, 1)
    text_grad = lax.dynamic_slice_in_dim(text_whole, feature_first, local_width, 1)
    return (loss_sum, emb_grad, text_grad)


def solution(mesh):
    placed = (
        P("dp", "mp"),
        P("dp"),
        P("dp"),
        P(None, "mp"),
        P("mp", None),
        P("dp", "mp"),
        P(),
        P(),
    )
    return jax.shard_map(
        shards,
        mesh=mesh,
        in_specs=placed,
        out_specs=(P("dp"), P("dp", "mp"), P("dp", "mp")),
        check_vma=False,
    )
```

profile of v0, /device:TPU:32, one launch (start us, length us, event | category | flops | bytes accessed | tf_op | source)
XLA Modules:
  0.0 948.0 jit_solution(8089313268084298118)
XLA Ops:
  7.2 0.0 copy-start
  7.2 0.0 all-gather.4.cloned.1.call-start
  7.2 0.7 all-gather.4.cloned.1.call-update
  7.9 0.0 reduce-scatter.2.cloned.1.call-start
  8.0 57.3 %all-gather.4.cloned.1.call-done = bf16[2048,1152]{0,1:T(8,128)(2,1)} async-done(((bf16[2048,288]{0,1:T(8,128)(2,1)}), bf16[2048,1152]{0,1:T(8,128)(2,1)}) %all-gather.4.cloned.1.call-update) | async-done | bytes 4718608 | tf_op jit(solution)/shard_map/all_gather | solution.py:29
  65.3 0.0 copy-start.1
  65.3 3.2 convert_reduce_fusion
  68.5 0.5 copy-done.1
  69.1 1.3 fusion.2
  70.3 0.0 copy-done
  70.3 19.9 %fusion.26 = f32[2048,1152]{1,0:T(8,128)} fusion(bf16[1076,1152]{1,0:T(8,128)(2,1)S(1)} %copy-done, bf16[1152,1076]{0,1:T(8,128)(2,1)} %param.11, bf16[2048,1152]{0,1:T(8,128)(2,1)} %all-gather.4.cloned.1.call-done, f32[2048]{0:T(1024)S(1)} %add_rsqrt_fusion, f32[2048]{0:T(1024)S(1)} %broadcast_multiply_fusion.1), kind=kOutput, calls=%fused_computation.29 | convolution fusion | flops 10183680000 | bytes 19130368 | tf_op jit(solution)/shard_map/dot_general | solution.py:33
  90.3 0.0 copy-start.5
  90.3 0.0 copy-start.4
  90.3 0.0 reduce-scatter.2.cloned.1.call-update
  90.3 0.0 all-reduce.3.cloned.1.call-start
  90.4 0.6 copy-done.5
  91.0 0.2 reduce-window.8
  91.1 0.0 copy-done.4
  91.1 5.1 all-gather
  96.3 0.1 reshape.77
  96.4 0.1 multiply_reduce_fusion.1
  96.5 0.1 convert_bitcast_fusion
  96.6 180.3 %all-gather.1 = bf16[64,2,1152]{2,1,0:T(2,128)(2,1)S(1)} all-gather(bf16[1,2,1152]{2,1,0:T(2,128)(2,1)S(1)} %get-tuple-element.7), channel_id=1, replica_groups=mesh['dp'=64,'mp'=4] {'dp'}, dimensions={0}, use_global_device_ids=true | all-gather | bytes 299520 | tf_op jit(solution)/shard_map/all_gather | solution.py:61
  276.9 0.1 reshape.76
  278.3 2.4 constant_dynamic-slice_fusion
  280.7 2.4 copy.17
  283.1 0.0 reduce-scatter.2.cloned.1.call-done
  283.1 0.0 copy-start.2
  283.1 0.0 copy-start.3
  283.1 2.4 fusion.28
  285.5 0.0 copy-start.6
  285.5 0.0 copy-start.7
  285.6 0.3 copy-done.2
  285.8 1.8 multiply_reduce_fusion
  287.6 0.0 copy-done.3
  287.6 1.2 fusion.18
  288.8 6.0 psum.7
  294.8 0.2 multiply_reduce_fusion.4
  295.0 0.1 broadcast_multiply_fusion
  295.1 0.0 copy-done.6
  295.1 0.9 fusion.41
  296.0 1.3 fusion.34
  297.3 0.0 all-reduce.3.cloned.1.call-update
  297.4 0.0 copy-done.7
  297.4 0.6 dynamic-slice
  298.6 0.4 multiply_reduce_fusion.3
  299.0 0.7 fusion.33
  299.7 640.2 %all-reduce.3.cloned.1.call-done = f32[128,1152]{1,0:T(8,128)} async-done(((f32[128,1152]{1,0:T(8,128)}), f32[128,1152]{1,0:T(8,128)}) %all-reduce.3.cloned.1.call-update) | async-done | bytes 589840
  939.9 0.9 multiply_reduce_fusion.2
  940.8 0.7 fusion.32
  (9 shorter events, 0.1 us)
Async XLA Ops:
  7.2 63.2 %copy-start = (bf16[1076,1152]{1,0:T(8,128)(2,1)S(1)}, bf16[1076,1152]{1,0:T(8,128)(2,1)}, u32[]{:S(2)}) copy-start(bf16[1076,1152]{1,0:T(8,128)(2,1)} %param.12) | copy-start | bytes 7437316
  7.2 58.1 %all-gather.4.cloned.1.call-start = ((), (), s32[]{:S(2)}) async-start(), calls=%async_computation.1 | async-start | bytes 5898240 | tf_op jit(solution)/shard_map/all_gather | solution.py:29
  7.9 275.2 %reduce-scatter.2.cloned.1.call-start = ((), (), s32[]{:S(2)}) async-start(), calls=%async_computation.2 | async-start | bytes 11796480 | tf_op jit(solution)/shard_map/reduce_scatter | solution.py:32
  65.3 3.8 copy-start.1
  90.3 0.7 copy-start.5
  90.3 0.8 copy-start.4
  90.3 849.6 %all-reduce.3.cloned.1.call-start = ((), (), s32[]{:S(2)}) async-start(), calls=%async_computation.3 | async-start | bytes 1179648
  283.1 2.7 copy-start.2
  283.1 4.5 copy-start.3
  285.5 9.6 %copy-start.6 = (s32[2]{0:T(128)S(1)}, s32[2]{0:T(128)}, u32[]{:S(2)}) copy-start(s32[2]{0:T(128)} %param.10) | copy-start | bytes 28
  285.5 11.8 %copy-start.7 = (u32[256]{0:T(256)S(1)}, u32[256]{0:T(256)}, u32[]{:S(2)}) copy-start(u32[256]{0:T(256)} %constant.49) | copy-start | bytes 3076
Sparse Core Ops, SparseCore 0:
  9.8 55.4 all-gather.3
  90.4 94.8 reduce-scatter.1
  297.5 642.3 all-reduce.2
where the time goes:
time: 948 us
  waiting for transfers between devices  698 us (74%)
  blocking collectives  191 us (20%)
  matrix products  23.8 us (3%)
  between operations  15.8 us (2%)
  other arithmetic  11.6 us (1%)
    unnamed x4, waiting for transfers between devices  641 us
    all_gather x1, blocking collectives, shards(): all_text = lax.all_gather(text_wire, 'dp', axis=0, tiled=True)  180 us
    all_gather x1, waiting for transfers between devices, shards(): full_rows = lax.all_gather(patches, 'mp', axis=1, tiled=True)  57.3 us
    dot_general x1, matrix products, shards(): jnp.dot(hidden, outer_weight, preferred_element_type=jnp.float32)  19.9 us
  transfers between devices with their start and end apart: 3, of which 2 were waited for; matrix products, arithmetic and copies ran while one was open for 1% of the time, Pallas kernels for 0%

commit v1 on v0

v1 whole, which is shorter than its diff:
```python
import functools

import jax
import jax.numpy as jnp
from jax import lax
from jax.experimental import pallas as pl
from jax.experimental.pallas import tpu as pltpu
from jax.sharding import PartitionSpec as P

MESH = pl.DeviceIdType.MESH
epsilon = 1e-06
D = 1152
DL = 288
F32, BF16 = jnp.float32, jnp.bfloat16


def layer_norm(values):
    centre = jnp.mean(values, axis=-1, keepdims=True)
    shifted = values - centre
    spread = jnp.mean(shifted * shifted, axis=-1, keepdims=True)
    return shifted * lax.rsqrt(spread + epsilon)


def expand_rows(normed, weights):
    return jax.nn.gelu(
        jnp.dot(normed, weights, preferred_element_type=jnp.float32), approximate=True
    )


def coords():
    dp, mp = lax.axis_index("dp"), lax.axis_index("mp")
    return dp // 16, (dp // 2) % 8, dp % 2, mp


def dp_of(x, z, yh):
    return x * 16 + z * 2 + yh


def tail_peers():
    x, z, yh, mp = coords()
    dp = dp_of(x, z, yh)
    group = [(dp, (mp + k) % 4) for k in range(1, 4)]
    line = [(dp_of(x, (z + k) % 8, yh), mp) for k in range(1, 8)]
    plane = [(dp_of((x + k // 2) % 4, z, (yh + k) % 2), mp) for k in range(1, 8)]
    return group, line, plane


def tail_body(
    counts_ref, pair_ref, scale_ref, bias_ref, loss_ref, emb_ref, txt_ref,
    sums, rows, packed, msg, dots, group_send, group_recv, line_send, line_recv,
    plane_send, plane_recv, dots_send, dots_recv,
):
    x, z, yh, mp = coords()
    group, line, plane = tail_peers()
    dp = dp_of(x, z, yh)
    slot = (x * 2 + yh) * 8 + z

    copies = []
    for k, peer in enumerate(group):
        copies.append(pltpu.make_async_remote_copy(
            src_ref=sums.at[mp], dst_ref=sums.at[mp], send_sem=group_send.at[k],
            recv_sem=group_recv.at[k], device_id=peer, device_id_type=MESH))
        copies[-1].start()
    for copy in copies:
        copy.wait_recv()
    total = ((sums[0] + sums[1]) + sums[2]) + sums[3]
    row = lax.broadcasted_iota(jnp.int32, (8, 1), 0)
    count = jnp.where(row == 0, counts_ref[0], jnp.where(row == 1, counts_ref[1], 1)).astype(F32)
    values = total / count
    norm = lax.rsqrt(jnp.sum(values * values, axis=1, keepdims=True) + epsilon)
    unit = values * norm
    rows[:, :D] = unit
    rows[:, D:] = jnp.zeros((8, rows.shape[1] - D), F32)
    lane = lax.broadcasted_iota(jnp.int32, (4, 128), 1)
    units = []
    for b in range(3):
        block = jnp.zeros((4, 128), F32)
        for k in range(4):
            block = jnp.where(mp == k, rows[0:4, DL * k + 128 * b: DL * k + 128 * b + 128], block)
        if b == 2:
            block = jnp.where(lane < DL - 256, block, 0.0)
        units.append(block)
        packed[4 * b:4 * b + 4, :] = block
    line4 = lax.broadcasted_iota(jnp.int32, (4, 128), 0)
    packed[12:16, :] = jnp.where(
        line4 == 0, pair_ref[0].astype(F32), jnp.where(line4 == 1, pair_ref[1].astype(F32), 0.0))
    msg[slot] = packed[...].astype(BF16)

    sends = []
    for k, peer in enumerate(line):
        sends.append(pltpu.make_async_remote_copy(
            src_ref=msg.at[slot], dst_ref=msg.at[slot], send_sem=line_send.at[k],
            recv_sem=line_recv.at[k], device_id=peer, device_id_type=MESH))
        sends[-1].start()
    row16 = lax.broadcasted_iota(jnp.int32, (16, 128), 0)
    lane16 = lax.broadcasted_iota(jnp.int32, (16, 128), 1)
    for b in range(3):
        wire = units[b].astype(BF16).astype(F32)
        packed[0:4, :] = wire
        packed[4:8, :] = units[b] - wire
        packed[8:16, :] = jnp.zeros((8, 128), F32)
        left = packed[...]
        if b == 0:
            left = jnp.where((row16 == 8) & (lane16 == 0), 1.0, left)
        rows_b = left.astype(BF16)
        lefts = [rows_b] if b == 0 else lefts + [rows_b]
    left = jnp.concatenate(lefts, axis=0)
    for copy in sends:
        copy.wait_recv()
    first = (x * 2 + yh) * 8
    for k, peer in enumerate(plane):
        sends.append(pltpu.make_async_remote_copy(
            src_ref=msg.at[pl.ds(first, 8)], dst_ref=msg.at[pl.ds(first, 8)], send_sem=plane_send.at[k],
            recv_sem=plane_recv.at[k], device_id=peer, device_id_type=MESH))
        sends[-1].start()
    for copy in sends[7:]:
        copy.wait_recv()
    everyone = msg[...].reshape(1024, 128)
    prod = lax.dot_general(left, everyone, (((1,), (1,)), ((), ())), preferred_element_type=F32)
    pairs = pltpu.roll(prod[0:16], 1024 - 12, 1)[8:9]
    part = prod[0:16] + pltpu.roll(prod[16:32], 1024 - 4, 1) + pltpu.roll(prod[32:48], 1024 - 8, 1)
    dots[mp] = part[0:8]
    swaps = []
    for k, peer in enumerate(group):
        swaps.append(pltpu.make_async_remote_copy(
            src_ref=dots.at[mp], dst_ref=dots.at[mp], send_sem=dots_send.at[k],
            recv_sem=dots_recv.at[k], device_id=peer, device_id_type=MESH))
        swaps[-1].start()
    for copy in swaps:
        copy.wait_recv()
    dot = ((dots[0] + dots[1]) + dots[2]) + dots[3]
    column = lax.broadcasted_iota(jnp.int32, (8, 1024), 1)
    place, kind = column // 16, column % 16
    shard = (place // 16) * 16 + (place % 8) * 2 + (place // 8) % 2
    row8 = lax.broadcasted_iota(jnp.int32, (8, 1024), 0)
    own_pair = jnp.where(row8 == 0, pair_ref[0], pair_ref[1])
    all_pair = jnp.broadcast_to(pairs, (8, 1024)).astype(jnp.int32)
    wanted = jnp.where(row8 < 2, own_pair, all_pair)
    match = wanted == jnp.where(row8 < 2, shard * 2 + kind - 2, dp * 2 + row8 - 2)
    valid = ((row8 < 2) & ((kind == 2) | (kind == 3))) | ((row8 >= 2) & (row8 < 4) & (kind < 2))
    scale = jnp.exp(jnp.full((8, 1024), scale_ref[0], F32))
    label = jnp.where(match, 1.0, -1.0)
    turned = -label * (scale * dot + bias_ref[0])
    small = jnp.exp(-jnp.abs(turned))
    soft = jnp.where(valid, jnp.maximum(turned, 0.0) + jnp.log1p(small), 0.0)
    sigmoid = jnp.where(turned >= 0, 1.0, small) / (1.0 + small)
    slope = jnp.where(valid, -label * sigmoid, 0.0)
    loss = jnp.sum(soft, axis=1, keepdims=True)
    whole = dot + pltpu.roll(dot, 4, 0)
    proj = jnp.sum(scale * slope * whole, axis=1, keepdims=True)[0:4]
    high = slope.astype(BF16)
    rest = slope - high.astype(F32)
    mid = rest.astype(BF16)
    low = (rest - mid.astype(F32)).astype(BF16)
    stack = jnp.concatenate([high.astype(F32), mid.astype(F32), low.astype(F32)], axis=0)
    stack = jnp.concatenate([stack, pltpu.roll(stack, 4, 1), pltpu.roll(stack, 8, 1)], axis=0).astype(BF16)
    dirs = jnp.dot(stack, everyone, preferred_element_type=F32)
    for b in range(3):
        own = dirs[24 * b:24 * b + 24]
        direction = (own[0:8] + (own[8:16] + own[16:24]))[0:4] * scale[0:4, 0:128]
        grad = (direction - units[b] * proj) * norm[0:4]
        width = 128 if b < 2 else DL - 256
        emb_ref[:, 128 * b:128 * b + width] = grad[0:2, :width]
        txt_ref[:, 128 * b:128 * b + width] = grad[2:4, :width]
    loss_ref[...] = jnp.broadcast_to(loss[0:2], (2, 128))
    for copy in copies + sends + swaps:
        copy.wait_send()


def tail_kernel(sum_ref, text_ref, counts_ref, pair_ref, scale_ref, bias_ref, loss_ref, emb_ref, txt_ref, *scratch):
    sums = scratch[0]
    mp = lax.axis_index("mp")
    barrier = pltpu.get_barrier_semaphore()
    group, line, plane = tail_peers()
    for peer in group + line + plane:
        pl.semaphore_signal(barrier, inc=1, device_id=peer, device_id_type=MESH)
    sums[mp] = jnp.zeros((8, D), F32)
    sums[mp, 0:2, :] = sum_ref[...]
    for k in range(4):
        @pl.when(mp == k)
        def _():
            sums[k, 2:4, DL * k:DL * k + DL] = text_ref[...].astype(F32)
    pl.semaphore_wait(barrier, 17)
    tail_body(counts_ref, pair_ref, scale_ref, bias_ref, loss_ref, emb_ref, txt_ref, *scratch)


def tail_scratch():
    dma = pltpu.SemaphoreType.DMA
    return [
        pltpu.VMEM((4, 8, D), F32),
        pltpu.VMEM((8, D + 128), F32),
        pltpu.VMEM((16, 128), F32),
        pltpu.VMEM((64, 16, 128), BF16),
        pltpu.VMEM((4, 8, 1024), F32),
        dma((3,)), dma((3,)), dma((7,)), dma((7,)), dma((7,)), dma((7,)), dma((3,)), dma((3,)),
    ]


def tail(sums, text, counts, pairs, log_scale, logit_bias):
    vmem, smem = pl.BlockSpec(memory_space=pltpu.VMEM), pl.BlockSpec(memory_space=pltpu.SMEM)
    loss, emb, txt = pl.pallas_call(
        tail_kernel,
        out_shape=(
            jax.ShapeDtypeStruct((2, 128), F32),
            jax.ShapeDtypeStruct((2, DL), F32),
            jax.ShapeDtypeStruct((2, DL), F32),
        ),
        in_specs=[vmem, vmem, smem, smem, smem, smem],
        out_specs=(vmem, vmem, vmem),
        scratch_shapes=tail_scratch(),
        compiler_params=pltpu.CompilerParams(collective_id=1, has_side_effects=True),
        name="tail",
    )(sums, text, counts, pairs, log_scale, logit_bias)
    return loss[:, 0], emb, txt


def shards(
    patches, counts, pair_ids, inner_weight, outer_weight, text_embed, log_scale, logit_bias
):
    group_size = lax.axis_size("mp")
    shard_rows = patches.shape[0]
    own_count = shard_rows // group_size
    row_first = lax.axis_index("mp") * own_count
    full_rows = lax.all_gather(patches, "mp", axis=1, tiled=True)
    normed = layer_norm(full_rows.astype(jnp.float32)).astype(jnp.bfloat16)
    hidden = expand_rows(normed, inner_weight).astype(jnp.bfloat16)
    mixed_rows = lax.psum_scatter(
        jnp.dot(hidden, outer_weight, preferred_element_type=jnp.float32),
        "mp",
        scatter_dimension=0,
        tiled=True,
    )
    own_rows = lax.dynamic_slice_in_dim(full_rows, row_first, own_count, 0)
    updated = own_rows.astype(jnp.float32) + mixed_rows
    final_rows = layer_norm(updated)
    row_ends = jnp.cumsum(counts)
    row_starts = row_ends - counts
    row_ids = row_first + jnp.arange(own_count, dtype=jnp.int32)
    member = (
        (row_ids[None, :] >= row_starts[:, None]) & (row_ids[None, :] < row_ends[:, None])
    ).astype(jnp.float32)
    partial_value = jnp.dot(member, final_rows, precision=lax.Precision.HIGHEST)
    return tail(partial_value, text_embed, counts, pair_ids, log_scale, logit_bias)


def solution(mesh):
    placed = (
        P("dp", "mp"),
        P("dp"),
        P("dp"),
        P(None, "mp"),
        P("mp", None),
        P("dp", "mp"),
        P(),
        P(),
    )
    return jax.shard_map(
        shards,
        mesh=mesh,
        in_specs=placed,
        out_specs=(P("dp"), P("dp", "mp"), P("dp", "mp")),
        check_vma=False,
    )
```

time: 948 us -> 226 us (0.24)
  the two profiles are of different devices: /device:TPU:32 before, /device:TPU:1 now
where the time goes in v1:
time: 226 us
  waiting for transfers between devices  145 us (64%)
  Pallas kernels  25.4 us (11%)
  matrix products  22 us (10%)
  between operations  15.4 us (7%)
  local copies, waits for them, and re-layouts  9.35 us (4%)
  other arithmetic  8.92 us (4%)
    reduce_scatter x1, waiting for transfers between devices, shards(): lax.psum_scatter(jnp.dot(hidden, outer_weight, preferred_element_type=jnp...  84.8 us
    all_gather x1, waiting for transfers between devices, shards(): full_rows = lax.all_gather(patches, 'mp', axis=1, tiled=True)  59.6 us
    pallas_call x1, Pallas kernels, tail(): pl.pallas_call(tail_kernel, out_shape=(jax.ShapeDtypeStruct((2, 128), F32...  25.4 us
    dot_general x1, matrix products, shards(): jnp.dot(hidden, outer_weight, preferred_element_type=jnp.float32)  20.1 us
    unnamed x13, local copies, waits for them, and re-layouts  5.68 us
    reduce_sum x2, other arithmetic, layer_norm(): centre = jnp.mean(values, axis=-1, keepdims=True)  5.65 us
  transfers between devices with their start and end apart: 2, of which 2 were waited for; matrix products, arithmetic and copies ran while one was open for 2% of the time, Pallas kernels for 0%

profile of v1, /device:TPU:1, one launch (start us, length us, event | category | flops | bytes accessed | tf_op | source)
XLA Modules:
  0.0 226.1 jit_solution(10482258665198855721)
XLA Ops:
  7.2 0.0 copy-start
  7.2 0.0 all-gather.2.cloned.1.call-start
  7.2 0.7 all-gather.2.cloned.1.call-update
  7.9 0.0 reduce-scatter.2.cloned.1.call-start
  8.0 59.6 %all-gather.2.cloned.1.call-done = bf16[2048,1152]{0,1:T(8,128)(2,1)} async-done(((bf16[2048,288]{0,1:T(8,128)(2,1)}), bf16[2048,1152]{0,1:T(8,128)(2,1)}) %all-gather.2.cloned.1.call-update) | async-done | bytes 4718608 | tf_op jit(solution)/shard_map/all_gather | solution.py:224
  67.5 0.0 copy-start.1
  67.5 3.2 %convert_reduce_fusion = f32[2048]{0:T(1024)S(1)} fusion(bf16[2048,1152]{0,1:T(8,128)(2,1)} %all-gather.2.cloned.1.call-done), kind=kLoop, calls=%fused_computation.2 | loop fusion | flops 4716544 | bytes 4726784 | tf_op jit(solution)/shard_map/reduce_sum | solution.py:18
  70.8 0.5 copy-done.1
  71.3 1.3 fusion.2
  72.6 0.0 copy-done
  72.6 20.1 %fusion.24 = f32[2048,1152]{1,0:T(8,128)} fusion(bf16[1076,1152]{1,0:T(8,128)(2,1)S(1)} %copy-done, bf16[1152,1076]{0,1:T(8,128)(2,1)} %param.11, bf16[2048,1152]{0,1:T(8,128)(2,1)} %all-gather.2.cloned.1.call-done, f32[2048]{0:T(1024)S(1)} %add_rsqrt_fusion, f32[2048]{0:T(1024)S(1)} %broadcast_multiply_fusion), kind=kOutput, calls=%fused_computation.25 | convolution fusion | flops 10183680000 | bytes 19130368 | tf_op jit(solution)/shard_map/dot_general | solution.py:228
  92.7 0.0 copy-start.4
  92.7 0.0 reduce-scatter.2.cloned.1.call-update
  94.0 0.0 copy-done.4
  94.0 0.2 reduce-window.8
  94.2 2.4 %constant_dynamic-slice_fusion = bf16[512,1152]{0,1:T(8,128)(2,1)} fusion(bf16[2048,1152]{0,1:T(8,128)(2,1)} %all-gather.2.cloned.1.call-done, s32[]{:T(128)S(6)} %select_n.3), kind=kLoop, calls=%fused_computation.39 | loop fusion | bytes 2359300 | tf_op jit(solution)/shard_map/dynamic_slice | solution.py:233
  96.6 2.4 %copy.14 = bf16[512,1152]{1,0:T(8,128)(2,1)} copy(bf16[512,1152]{0,1:T(8,128)(2,1)} %constant_dynamic-slice_fusion) | data formatting | bytes 2359296
  99.0 84.8 %reduce-scatter.2.cloned.1.call-done = f32[512,1152]{1,0:T(8,128)} async-done(((f32[2048,1152]{1,0:T(8,128)}), f32[512,1152]{1,0:T(8,128)}) %reduce-scatter.2.cloned.1.call-update) | async-done | bytes 2359312 | tf_op jit(solution)/shard_map/reduce_scatter | solution.py:227
  183.7 0.0 copy-start.2
  183.7 0.0 copy-start.3
  183.7 2.4 %fusion.26 = f32[512]{0:T(512)S(1)} fusion(f32[512,1152]{1,0:T(8,128)} %reduce-scatter.2.cloned.1.call-done, bf16[512,1152]{1,0:T(8,128)(2,1)} %copy.14), kind=kLoop, calls=%fused_computation.26 | loop fusion | flops 1768960 | bytes 3540992 | tf_op jit(solution)/shard_map/reduce_sum | solution.py:18
  186.2 0.3 copy-done.2
  186.5 1.8 multiply_reduce_fusion
  188.3 0.0 copy-done.3
  188.3 1.8 fusion.18.sum_ref
  190.1 25.4 %tail.1 = (f32[2,128]{1,0:T(2,128)}, f32[2,288]{1,0:T(2,128)}, f32[2,288]{1,0:T(2,128)}) custom-call(f32[2,1152]{1,0:T(2,128)} %fusion.18.sum_ref, bf16[2,288]{1,0:T(2,128)(2,1)} %text_ref.1, s32[2]{0:T(128)} %counts_ref.1, s32[2]{0:T(128)} %pair_ref.1, f32[1]{0:T(128)S(6)} %copy.17.scale_ref, f32[1]{0:T(128)S(6)} %copy.18.bias_ref), custom_call_target="tpu_custom_call" | custom-call | tf_op jit(solution)/shard_map/tail/pallas_call | solution.py:201
  215.5 1.3 slice_reduce_fusion
  216.8 1.2 copy.19
  218.0 1.2 copy.20
  (6 shorter events, 0.0 us)
Async XLA Ops:
  7.2 65.4 %copy-start = (bf16[1076,1152]{1,0:T(8,128)(2,1)S(1)}, bf16[1076,1152]{1,0:T(8,128)(2,1)}, u32[]{:S(2)}) copy-start(bf16[1076,1152]{1,0:T(8,128)(2,1)} %param.12) | copy-start | bytes 7437316
  7.2 60.4 %all-gather.2.cloned.1.call-start = ((), (), s32[]{:S(2)}) async-start(), calls=%async_computation.1 | async-start | bytes 5898240 | tf_op jit(solution)/shard_map/all_gather | solution.py:224
  7.9 175.8 %reduce-scatter.2.cloned.1.call-start = ((), (), s32[]{:S(2)}) async-start(), calls=%async_computation.2 | async-start | bytes 11796480 | tf_op jit(solution)/shard_map/reduce_scatter | solution.py:227
  67.5 3.8 %copy-start.1 = (bf16[2048,1152]{0,1:T(8,128)(2,1)S(1)}, bf16[2048,1152]{0,1:T(8,128)(2,1)}, u32[]{:S(2)}) copy-start(bf16[2048,1152]{0,1:T(8,128)(2,1)} %all-gather.2.cloned.1.call-done) | copy-start | bytes 14155780
  92.7 1.3 copy-start.4
  183.7 2.7 %copy-start.2 = (f32[512,1152]{1,0:T(8,128)S(1)}, f32[512,1152]{1,0:T(8,128)}, u32[]{:S(2)}) copy-start(f32[512,1152]{1,0:T(8,128)} %reduce-scatter.2.cloned.1.call-done) | copy-start | bytes 7077892
  183.7 4.5 %copy-start.3 = (bf16[512,1152]{1,0:T(8,128)(2,1)S(1)}, bf16[512,1152]{1,0:T(8,128)(2,1)}, u32[]{:S(2)}) copy-start(bf16[512,1152]{1,0:T(8,128)(2,1)} %copy.14) | copy-start | bytes 3538948
Sparse Core Ops, SparseCore 0:
  9.8 57.6 all-gather.1
  92.9 90.8 reduce-scatter.1

commit v2 on v1

--- a/solution.py
+++ b/solution.py
@@ -12,19 +12,6 @@
 D = 1152
 DL = 288
 F32, BF16 = jnp.float32, jnp.bfloat16
-
-
-def layer_norm(values):
-    centre = jnp.mean(values, axis=-1, keepdims=True)
-    shifted = values - centre
-    spread = jnp.mean(shifted * shifted, axis=-1, keepdims=True)
-    return shifted * lax.rsqrt(spread + epsilon)
-
-
-def expand_rows(normed, weights):
-    return jax.nn.gelu(
-        jnp.dot(normed, weights, preferred_element_type=jnp.float32), approximate=True
-    )
 
 
 def coords():
@@ -214,33 +201,291 @@
     return loss[:, 0], emb, txt
 
 
+ROWS = 512
+MAIN = 1024
+TAIL = 64
+LINK = {}
+for _s in range(10):
+    for _k in range(2):
+        LINK[_s, _k] = "hi" if _s < 5 else ("hi", "lo")[_k]
+
+
+def stage_rows(stage):
+    local = stage % 5
+    return (0, 16) if local == 0 else (128 + 256 * (local - 1), 32)
+
+
+def main_peers():
+    x, z, yh, mp = coords()
+    dp = dp_of(x, z, yh)
+    return dict(
+        core=(dp, mp + 1 - 2 * (mp % 2)),
+        lo=(dp, (mp + 2) % 4),
+        cross=(dp, 3 - mp),
+        hi=(dp + 1 - 2 * (dp % 2), (mp + 2) % 4),
+        xp=(dp_of((x + 1) % 4, z, yh), mp),
+        xm=(dp_of((x + 3) % 4, z, yh), mp),
+        zp=(dp_of(x, (z + 1) % 8, yh), mp),
+        zm=(dp_of(x, (z + 7) % 8, yh), mp),
+    )
+
+
+def gelu(u):
+    inner = u * (0.7978845608028654 + 0.035677408136300125 * (u * u))
+    half = 0.5 * u
+    return half + half * jnp.tanh(inner)
+
+
+def main_kernel(
+    patch_ref, inner_ref, outer_ref, tail_ref, counts_ref, out_ref,
+    w1_own, w2_own, w1_oth, w2_oth, xin, xres, xn, acc, hid, hid_oth, part_out, part_in,
+    load_sem, own_sem, patch_send, patch_recv, norm_send, norm_recv, y_send, y_recv,
+    side_send, side_recv, part_send, part_recv,
+):
+    x, z, yh, mp = coords()
+    dp = dp_of(x, z, yh)
+    core = mp % 2
+    colour = [(x + 2 * z) % 4, (2 * x + z) % 4]
+    peers = main_peers()
+    barrier = pltpu.get_barrier_semaphore()
+    for peer in peers.values():
+        pl.semaphore_signal(barrier, inc=1, device_id=peer, device_id_type=MESH)
+    loads = [
+        pltpu.make_async_copy(inner_ref.at[:, pl.ds(0, MAIN)], w1_own, load_sem.at[0]),
+        pltpu.make_async_copy(outer_ref.at[pl.ds(0, MAIN)], w2_own.at[pl.ds(128, MAIN)], load_sem.at[1]),
+        pltpu.make_async_copy(tail_ref, w2_own.at[pl.ds(0, 128)], load_sem.at[2]),
+    ]
+    mine = pltpu.make_async_copy(patch_ref.at[pl.ds(pl.multiple_of(ROWS * mp, ROWS), ROWS)], xin.at[mp], own_sem)
+    mine.start()
+    loads[2].start()
+    loads[0].start()
+    loads[1].start()
+    pl.semaphore_wait(barrier, len(peers))
+
+    def patch_copy(rb, k):
+        who = (mp + k) % 4
+        return pltpu.make_async_remote_copy(
+            src_ref=patch_ref.at[pl.ds(pl.multiple_of(ROWS * who + 128 * rb, 128), 128)],
+            dst_ref=xin.at[mp, pl.ds(pl.multiple_of(128 * rb, 128), 128)],
+            send_sem=patch_send.at[rb, k - 1], recv_sem=patch_recv.at[rb, k - 1],
+            device_id=(dp, who), device_id_type=MESH)
+
+    def start_patches(rb):
+        for k in range(1, 4):
+            patch_copy(rb, k).start()
+
+    def piece(stage, kind, base=None, rows=None):
+        if base is None:
+            base, rows = stage_rows(stage)
+        return pl.ds(pl.multiple_of(base + (kind * 4 + colour[kind]) * rows, 16), rows)
+
+    def y_copy(stage, kind):
+        rows = piece(stage, kind)
+        src, dst = (w1_own, w1_oth) if stage < 5 else (w2_own, w2_oth)
+        return pltpu.make_async_remote_copy(
+            src_ref=src.at[rows], dst_ref=dst.at[rows],
+            send_sem=y_send.at[stage, kind], recv_sem=y_recv.at[stage, kind],
+            device_id=peers[LINK[stage, kind]], device_id_type=MESH)
+
+    def side_copy(stage, kind, j, dst, base=None, rows=None):
+        turn = 1 - 2 * (stage % 2)
+        strong = ("xp", "xm") if kind == 0 else ("zp", "zm")
+        if j < 2:
+            who = peers[strong[j]]
+        elif kind == 0:
+            who = (dp_of(x, (z + turn + 8) % 8, yh), mp)
+        else:
+            who = (dp_of((x + turn + 4) % 4, z, yh), mp)
+        rows = piece(stage, kind, base, rows)
+        return pltpu.make_async_remote_copy(
+            src_ref=dst.at[rows], dst_ref=dst.at[rows],
+            send_sem=side_send.at[stage, kind, j], recv_sem=side_recv.at[stage, kind, j],
+            device_id=who, device_id_type=MESH)
+
+    def forward(stage, dst, base, rows):
+        for kind in range(2):
+            at = piece(stage, kind, base, rows)
+            pltpu.make_async_remote_copy(
+                src_ref=dst.at[at], dst_ref=dst.at[at], send_sem=y_send.at[stage, kind],
+                recv_sem=y_recv.at[stage, kind], device_id=peers["hi"], device_id_type=MESH).wait_recv()
+            for j in range(3):
+                side_copy(stage, kind, j, dst, base, rows).start()
+
+    def arrive(stage, dst, base, rows):
+        for kind in range(2):
+            for j in range(3):
+                side_copy(stage, kind, j, dst, base, rows).wait_recv()
+
+    start_patches(0)
+    loads[2].wait()
+    loads[0].wait()
+    for stage in range(5):
+        for kind in range(2):
+            y_copy(stage, kind).start()
+        if stage < 3:
+            start_patches(stage + 1)
+    loads[1].wait()
+    for stage in range(5, 10):
+        for kind in range(2):
+            y_copy(stage, kind).start()
+    forward(0, w1_oth, 0, 16)
+    mine.wait()
+
+    def norm_copy(rb):
+        return pltpu.make_async_remote_copy(
+            src_ref=xn.at[rb, core], dst_ref=xn.at[rb, core],
+            send_sem=norm_send.at[rb], recv_sem=norm_recv.at[rb],
+            device_id=peers["core"], device_id_type=MESH)
+
+    def normalise(rb):
+        for k in range(1, 4):
+            patch_copy(rb, k).wait_recv()
+        rows = pl.ds(pl.multiple_of(128 * rb, 128), 128)
+        parts = [xin[m, rows, :] for m in range(4)]
+        wide = [part.astype(F32) for part in parts]
+        centre = sum(jnp.sum(part, axis=1, keepdims=True) for part in wide) * (1.0 / D)
+        wide = [part - centre for part in wide]
+        spread = sum(jnp.sum(part * part, axis=1, keepdims=True) for part in wide) * (1.0 / D)
+        scale = lax.rsqrt(spread + epsilon)
+        for m in range(4):
+            xres[rows, DL * m:DL * m + DL] = parts[m]
+            xn[rb, core, :, DL * m:DL * m + DL] = (wide[m] * scale).astype(BF16)
+        norm_copy(rb).start()
+
+    def own(rb):
+        norm_copy(rb).wait_recv()
+        block = xn[rb].reshape(256, D)
+        for j in range(4):
+            hid[:, 256 * j:256 * j + 256] = gelu(
+                jnp.dot(block, w1_own[:, 256 * j:256 * j + 256], preferred_element_type=F32)).astype(BF16)
+        acc[rb] = jnp.dot(hid[...], w2_own[128:, :], preferred_element_type=F32).reshape(2, 128, D)
+
+    def first(rb, _):
+        forward(rb + 1, w1_oth, pl.multiple_of(128 + 256 * rb, 128), 32)
+        normalise(rb)
+
+        @pl.when(rb > 0)
+        def _():
+            own(rb - 1)
+        return 0
+    lax.fori_loop(0, 4, first, 0)
+    forward(5, w2_oth, 0, 16)
+    own(3)
+    arrive(0, w1_oth, 0, 16)
+    def wait_inner(s, _):
+        arrive(s + 1, w1_oth, pl.multiple_of(128 + 256 * s, 128), 32)
+        return 0
+    lax.fori_loop(0, 4, wait_inner, 0)
+
+    def second(rb, _):
+        block = xn[rb].reshape(256, D)
+        for j in range(4):
+            hid_oth[rb, :, 256 * j:256 * j + 256] = gelu(
+                jnp.dot(block, w1_oth[:, 256 * j:256 * j + 256], preferred_element_type=F32)).astype(BF16)
+        forward(rb + 6, w2_oth, pl.multiple_of(128 + 256 * rb, 128), 32)
+        return 0
+    lax.fori_loop(0, 4, second, 0)
+
+    arrive(5, w2_oth, 0, 16)
+    tail_in = jnp.concatenate([w2_own[0:TAIL, :], w2_oth[0:TAIL, :]], axis=0)
+    tail_out = jnp.concatenate([w2_own[TAIL:2 * TAIL, :], w2_oth[TAIL:2 * TAIL, :]], axis=0)
+
+    def tails(rb, _):
+        block = xn[rb].reshape(256, D)
+        units = gelu(lax.dot_general(block, tail_in, (((1,), (1,)), ((), ())), preferred_element_type=F32)).astype(BF16)
+        acc[rb] += jnp.dot(units, tail_out, preferred_element_type=F32).reshape(2, 128, D)
+        return 0
+    lax.fori_loop(0, 4, tails, 0)
+
+    for s in range(4):
+        arrive(s + 6, w2_oth, 128 + 256 * s, 32)
+
+        def mix(rb, _):
+            acc[rb] += jnp.dot(
+                hid_oth[rb, :, 256 * s:256 * s + 256], w2_oth[128 + 256 * s:384 + 256 * s, :],
+                preferred_element_type=F32).reshape(2, 128, D)
+            if s == 3:
+                part_out[rb] = acc[rb, 1 - core].astype(BF16)
+                part_copy(rb).start()
+            return 0
+
+        def part_copy(rb):
+            return pltpu.make_async_remote_copy(
+                src_ref=part_out.at[rb], dst_ref=part_in.at[rb], send_sem=part_send.at[rb],
+                recv_sem=part_recv.at[rb], device_id=peers["core"], device_id_type=MESH)
+        lax.fori_loop(0, 4, mix, 0)
+
+    n0 = counts_ref[0]
+    n1 = n0 + counts_ref[1]
+
+    def finish(rb, sums):
+        part_copy(rb).wait_recv()
+        rows = pl.ds(pl.multiple_of(128 * rb, 128), 128)
+        value = xres[rows, :].astype(F32) + (acc[rb, core] + part_in[rb].astype(F32))
+        shifted = value - jnp.sum(value, axis=1, keepdims=True) * (1.0 / D)
+        spread = jnp.sum(shifted * shifted, axis=1, keepdims=True) * (1.0 / D)
+        scale = lax.rsqrt(spread + epsilon)
+        ids = ROWS * mp + 128 * rb + lax.broadcasted_iota(jnp.int32, (128, 1), 0)
+        normed = shifted * scale
+        a = jnp.sum(jnp.where(ids < n0, normed, 0.0), axis=0, keepdims=True)
+        b = jnp.sum(jnp.where((ids >= n0) & (ids < n1), normed, 0.0), axis=0, keepdims=True)
+        return sums[0] + a, sums[1] + b
+    zero = jnp.zeros((1, D), F32)
+    a, b = lax.fori_loop(0, 4, finish, (zero, zero))
+    out_ref[0:1, :] = a
+    out_ref[1:2, :] = b
+
+    def drain(rb, _):
+        for k in range(1, 4):
+            patch_copy(rb, k).wait_send()
+        norm_copy(rb).wait_send()
+        part_copy(rb).wait_send()
+        return 0
+    lax.fori_loop(0, 4, drain, 0)
+    for stage in range(10):
+        dst = w1_oth if stage < 5 else w2_oth
+        for kind in range(2):
+            y_copy(stage, kind).wait_send()
+            for j in range(3):
+                side_copy(stage, kind, j, dst).wait_send()
+
+
+def main_scratch():
+    dma = pltpu.SemaphoreType.DMA
+    return [
+        pltpu.VMEM((D, MAIN), BF16), pltpu.VMEM((D, D), BF16),
+        pltpu.VMEM((D, MAIN), BF16), pltpu.VMEM((D, D), BF16),
+        pltpu.VMEM((4, ROWS, DL), BF16), pltpu.VMEM((ROWS, D), BF16),
+        pltpu.VMEM((4, 2, 128, D), BF16), pltpu.VMEM((4, 2, 128, D), F32),
+        pltpu.VMEM((256, MAIN), BF16), pltpu.VMEM((4, 256, MAIN), BF16),
+        pltpu.VMEM((4, 128, D), BF16), pltpu.VMEM((4, 128, D), BF16),
+        dma((3,)), dma, dma((4, 3)), dma((4, 3)), dma((4,)), dma((4,)), dma((10, 2)), dma((10, 2)),
+        dma((10, 2, 3)), dma((10, 2, 3)), dma((4,)), dma((4,)),
+    ]
+
+
+def image_sums(patches, inner, outer, counts):
+    blank = jnp.zeros((TAIL - (inner.shape[1] - MAIN), D), BF16)
+    tails = jnp.concatenate([inner[:, MAIN:].T, blank, outer[MAIN:], blank], axis=0)
+    vmem, smem = pl.BlockSpec(memory_space=pltpu.VMEM), pl.BlockSpec(memory_space=pltpu.SMEM)
+    hbm = pl.BlockSpec(memory_space=pl.ANY)
+    return pl.pallas_call(
+        main_kernel,
+        out_shape=jax.ShapeDtypeStruct((2, D), F32),
+        in_specs=[hbm, hbm, hbm, hbm, smem],
+        out_specs=vmem,
+        scratch_shapes=main_scratch(),
+        compiler_params=pltpu.CompilerParams(
+            collective_id=2, has_side_effects=True, vmem_limit_bytes=56 * 2**20),
+        name="tower",
+    )(patches, inner, outer, tails, counts)
+
+
 def shards(
     patches, counts, pair_ids, inner_weight, outer_weight, text_embed, log_scale, logit_bias
 ):
-    group_size = lax.axis_size("mp")
-    shard_rows = patches.shape[0]
-    own_count = shard_rows // group_size
-    row_first = lax.axis_index("mp") * own_count
-    full_rows = lax.all_gather(patches, "mp", axis=1, tiled=True)
-    normed = layer_norm(full_rows.astype(jnp.float32)).astype(jnp.bfloat16)
-    hidden = expand_rows(normed, inner_weight).astype(jnp.bfloat16)
-    mixed_rows = lax.psum_scatter(
-        jnp.dot(hidden, outer_weight, preferred_element_type=jnp.float32),
-        "mp",
-        scatter_dimension=0,
-        tiled=True,
-    )
-    own_rows = lax.dynamic_slice_in_dim(full_rows, row_first, own_count, 0)
-    updated = own_rows.astype(jnp.float32) + mixed_rows
-    final_rows = layer_norm(updated)
-    row_ends = jnp.cumsum(counts)
-    row_starts = row_ends - counts
-    row_ids = row_first + jnp.arange(own_count, dtype=jnp.int32)
-    member = (
-        (row_ids[None, :] >= row_starts[:, None]) & (row_ids[None, :] < row_ends[:, None])
-    ).astype(jnp.float32)
-    partial_value = jnp.dot(member, final_rows, precision=lax.Precision.HIGHEST)
-    return tail(partial_value, text_embed, counts, pair_ids, log_scale, logit_bias)
+    sums = image_sums(patches, inner_weight, outer_weight, counts)
+    return tail(sums, text_embed, counts, pair_ids, log_scale, logit_bias)
 
 
 def solution(mesh):

time: 226 us -> 89.5 us (0.40)
  waiting for transfers between devices: 145 us -> 0 us
  Pallas kernels: 25.4 us -> 75 us
  matrix products: 22 us -> 0 us
  between operations: 15.4 us -> 2.11 us
  other arithmetic: 8.92 us -> 0.74 us
    reduce_scatter x1 -> x0, waiting for transfers between devices: 84.8 us -> none  [shards(): lax.psum_scatter(jnp.dot(hidden, outer_weight, preferred_element_type=jnp...]
    all_gather x1 -> x0, waiting for transfers between devices: 59.6 us -> none  [shards(): full_rows = lax.all_gather(patches, 'mp', axis=1, tiled=True)]
    pallas_call x0 -> x1, Pallas kernels: none -> 52.2 us  [image_sums(): pl.pallas_call(main_kernel, out_shape=jax.ShapeDtypeStruct((2, D), F32),...]
    dot_general x2 -> x0, matrix products: 22 us -> none  [the longest x1 20.1 us: shards(): jnp.dot(hidden, outer_weight, preferred_element_type=jnp.float32)]
    reduce_sum x4 -> x0, other arithmetic: 8.71 us -> none  [the longest x2 5.65 us: layer_norm(): centre = jnp.mean(values, axis=-1, keepdims=True)]
    pallas_call x1, Pallas kernels: 25.4 us -> 22.7 us  [tail(): pl.pallas_call(tail_kernel, out_shape=(jax.ShapeDtypeStruct((2, 128), F32...]
    unnamed x13 -> x6, local copies, waits for them, and re-layouts: 5.68 us -> 8.31 us
    dynamic_slice x1 -> x0, local copies, waits for them, and re-layouts: 2.38 us -> none  [shards(): own_rows = lax.dynamic_slice_in_dim(full_rows, row_first, own_count, 0)]
  transfers between devices with their start and end apart: 2 -> 0, of which waited for: 2 -> 0; matrix products, arithmetic and copies ran while one was open for 2% -> 0% of each run, Pallas kernels for 0% -> 0%
where the time goes in v2:
time: 89.5 us; the launch traced here: 89.2 us
  Pallas kernels  75 us (84%)
  local copies, waits for them, and re-layouts  11.4 us (13%)
  between operations  2.11 us (2%)
    pallas_call x1, Pallas kernels, image_sums(): pl.pallas_call(main_kernel, out_shape=jax.ShapeDtypeStruct((2, D), F32),...  52.2 us
    pallas_call x1, Pallas kernels, tail(): pl.pallas_call(tail_kernel, out_shape=(jax.ShapeDtypeStruct((2, 128), F32...  22.7 us
    unnamed x6, local copies, waits for them, and re-layouts  8.31 us

profile of v2, /device:TPU:1, one launch (start us, length us, event | category | flops | bytes accessed | tf_op | source)
XLA Modules:
  0.0 89.2 jit_solution(356776980634546635)
XLA Ops:
  0.6 0.0 copy-start
  2.1 0.9 %slice_bitcast_fusion = bf16[52,1152]{1,0:T(8,128)(2,1)S(1)} fusion(bf16[1152,1076]{0,1:T(8,128)(2,1)} %param.11), kind=kLoop, calls=%fused_computation.1 | loop fusion | bytes 239616 | tf_op jit(solution)/shard_map/transpose | solution.py:469
  3.0 0.9 %slice.10 = bf16[52,1152]{1,0:T(8,128)(2,1)S(1)} slice(bf16[1076,1152]{1,0:T(8,128)(2,1)} %outer_ref.1), slice={[1024:1076], [0:1152]} | slice | bytes 239616 | tf_op jit(solution)/shard_map/slice | solution.py:469
  3.9 0.7 pad_maximum_fusion.tail_ref
  4.7 2.5 %copy.13.patch_ref = bf16[2048,288]{1,0:T(8,128)(2,1)} copy(bf16[2048,288]{0,1:T(8,128)(2,1)} %param.8) | data formatting | bytes 2359296 | tf_op args[0]
  7.2 0.0 copy-done
  7.2 3.3 %copy.14.inner_ref = bf16[1152,1076]{1,0:T(8,128)(2,1)} copy(bf16[1152,1076]{0,1:T(8,128)(2,1)S(1)} %copy-done) | data formatting | bytes 4958208 | tf_op args[3]
  10.5 52.2 %tower.1.sum_ref = f32[2,1152]{1,0:T(2,128)} custom-call(bf16[2048,288]{1,0:T(8,128)(2,1)} %copy.13.patch_ref, bf16[1152,1076]{1,0:T(8,128)(2,1)} %copy.14.inner_ref, bf16[1076,1152]{1,0:T(8,128)(2,1)} %outer_ref.1, bf16[128,1152]{1,0:T(8,128)(2,1)} %pad_maximum_fusion.tail_ref, s32[2]{0:T(128)} %counts_ref.3), custom_call_target="tpu_custom_call" | custom-call | tf_op jit(solution)/shard_map/tower/pallas_call | solution.py:472
  62.7 22.7 %tail.1 = (f32[2,128]{1,0:T(2,128)}, f32[2,288]{1,0:T(2,128)}, f32[2,288]{1,0:T(2,128)}) custom-call(f32[2,1152]{1,0:T(2,128)} %tower.1.sum_ref, bf16[2,288]{1,0:T(2,128)(2,1)} %text_ref.1, s32[2]{0:T(128)} %counts_ref.3, s32[2]{0:T(128)} %pair_ref.1, f32[1]{0:T(128)S(6)} %copy.17.scale_ref, f32[1]{0:T(128)S(6)} %copy.18.bias_ref), custom_call_target="tpu_custom_call" | custom-call | tf_op jit(solution)/shard_map/tail/pallas_call | solution.py:188
  85.5 1.3 %slice_reduce_fusion = f32[2]{0:T(128)} fusion(f32[2,128]{1,0:T(2,128)} %get-tuple-element.6), kind=kLoop, calls=%fused_computation.2 | loop fusion | bytes 16 | tf_op jit(solution)/shard_map/slice | solution.py:201
  86.7 1.3 %copy.19 = f32[2,288]{1,0:T(2,128)} copy(f32[2,288]{1,0:T(2,128)} %get-tuple-element.13) | data formatting | bytes 4608
  88.0 1.2 %copy.20 = f32[2,288]{1,0:T(2,128)} copy(f32[2,288]{1,0:T(2,128)} %get-tuple-element.14) | data formatting | bytes 4608
  (1 shorter events, 0.0 us)
Async XLA Ops:
  0.6 6.6 %copy-start = (bf16[1152,1076]{0,1:T(8,128)(2,1)S(1)}, bf16[1152,1076]{0,1:T(8,128)(2,1)}, u32[]{:S(2)}) copy-start(bf16[1152,1076]{0,1:T(8,128)(2,1)} %param.11) | copy-start | bytes 7437316

commit v3 on v1

--- a/solution.py
+++ b/solution.py
@@ -12,19 +12,6 @@
 D = 1152
 DL = 288
 F32, BF16 = jnp.float32, jnp.bfloat16
-
-
-def layer_norm(values):
-    centre = jnp.mean(values, axis=-1, keepdims=True)
-    shifted = values - centre
-    spread = jnp.mean(shifted * shifted, axis=-1, keepdims=True)
-    return shifted * lax.rsqrt(spread + epsilon)
-
-
-def expand_rows(normed, weights):
-    return jax.nn.gelu(
-        jnp.dot(normed, weights, preferred_element_type=jnp.float32), approximate=True
-    )
 
 
 def coords():
@@ -48,7 +35,7 @@
 def tail_body(
     counts_ref, pair_ref, scale_ref, bias_ref, loss_ref, emb_ref, txt_ref,
     sums, rows, packed, msg, dots, group_send, group_recv, line_send, line_recv,
-    plane_send, plane_recv, dots_send, dots_recv,
+    plane_send, plane_recv, dots_send, dots_recv, meanwhile,
 ):
     x, z, yh, mp = coords()
     group, line, plane = tail_peers()
@@ -61,6 +48,7 @@
             src_ref=sums.at[mp], dst_ref=sums.at[mp], send_sem=group_send.at[k],
             recv_sem=group_recv.at[k], device_id=peer, device_id_type=MESH))
         copies[-1].start()
+    meanwhile()
     for copy in copies:
         copy.wait_recv()
     total = ((sums[0] + sums[1]) + sums[2]) + sums[3]
@@ -167,23 +155,6 @@
         copy.wait_send()
 
 
-def tail_kernel(sum_ref, text_ref, counts_ref, pair_ref, scale_ref, bias_ref, loss_ref, emb_ref, txt_ref, *scratch):
-    sums = scratch[0]
-    mp = lax.axis_index("mp")
-    barrier = pltpu.get_barrier_semaphore()
-    group, line, plane = tail_peers()
-    for peer in group + line + plane:
-        pl.semaphore_signal(barrier, inc=1, device_id=peer, device_id_type=MESH)
-    sums[mp] = jnp.zeros((8, D), F32)
-    sums[mp, 0:2, :] = sum_ref[...]
-    for k in range(4):
-        @pl.when(mp == k)
-        def _():
-            sums[k, 2:4, DL * k:DL * k + DL] = text_ref[...].astype(F32)
-    pl.semaphore_wait(barrier, 17)
-    tail_body(counts_ref, pair_ref, scale_ref, bias_ref, loss_ref, emb_ref, txt_ref, *scratch)
-
-
 def tail_scratch():
     dma = pltpu.SemaphoreType.DMA
     return [
@@ -196,51 +167,298 @@
     ]
 
 
-def tail(sums, text, counts, pairs, log_scale, logit_bias):
-    vmem, smem = pl.BlockSpec(memory_space=pltpu.VMEM), pl.BlockSpec(memory_space=pltpu.SMEM)
-    loss, emb, txt = pl.pallas_call(
-        tail_kernel,
-        out_shape=(
-            jax.ShapeDtypeStruct((2, 128), F32),
-            jax.ShapeDtypeStruct((2, DL), F32),
-            jax.ShapeDtypeStruct((2, DL), F32),
-        ),
-        in_specs=[vmem, vmem, smem, smem, smem, smem],
-        out_specs=(vmem, vmem, vmem),
-        scratch_shapes=tail_scratch(),
-        compiler_params=pltpu.CompilerParams(collective_id=1, has_side_effects=True),
-        name="tail",
-    )(sums, text, counts, pairs, log_scale, logit_bias)
-    return loss[:, 0], emb, txt
+ROWS = 512
+MAIN = 1024
+TAIL = 64
+WINDOW = 2
+STAGES = 9
+LINK = {}
+for _s in range(STAGES):
+    for _k in range(2):
+        LINK[_s, _k] = "hi" if _s < 5 else ("hi", "lo")[_k]
+
+
+def main_peers():
+    x, z, yh, mp = coords()
+    dp = dp_of(x, z, yh)
+    return dict(
+        core=(dp, mp + 1 - 2 * (mp % 2)),
+        lo=(dp, (mp + 2) % 4),
+        cross=(dp, 3 - mp),
+        hi=(dp + 1 - 2 * (dp % 2), (mp + 2) % 4),
+        xp=(dp_of((x + 1) % 4, z, yh), mp),
+        xm=(dp_of((x + 3) % 4, z, yh), mp),
+        zp=(dp_of(x, (z + 1) % 8, yh), mp),
+        zm=(dp_of(x, (z + 7) % 8, yh), mp),
+    )
+
+
+def gelu(u):
+    inner = u * (0.7978845608028654 + 0.035677408136300125 * (u * u))
+    half = 0.5 * u
+    return half + half * jnp.tanh(inner)
+
+
+def main_kernel(
+    patch_ref, inner_ref, outer_ref, inner_tail, outer_tail, text_ref, counts_ref, pair_ref, scale_ref, bias_ref,
+    loss_ref, emb_ref, txt_ref,
+    w1_own, w2_own, w1_oth, w2_oth, xin, xres, xn, acc, hid, part_out, part_in,
+    load_sem, own_sem, patch_send, patch_recv, norm_send, norm_recv, y_send, y_recv,
+    side_send, side_recv, part_send, part_recv, *tail_refs,
+):
+    x, z, yh, mp = coords()
+    dp = dp_of(x, z, yh)
+    core = mp % 2
+    colour = [(x + 2 * z) % 4, (2 * x + z) % 4]
+    peers = main_peers()
+    barrier = pltpu.get_barrier_semaphore()
+    group, line, plane = tail_peers()
+    everyone = [peers["hi"]] + group + line + plane
+    for peer in everyone:
+        pl.semaphore_signal(barrier, inc=1, device_id=peer, device_id_type=MESH)
+    mains = pl.ds(2 * TAIL, MAIN)
+    loads = [
+        pltpu.make_async_copy(inner_ref.at[pl.ds(0, MAIN)], w1_own.at[mains], load_sem.at[0]),
+        pltpu.make_async_copy(outer_ref.at[pl.ds(0, MAIN)], w2_own.at[mains], load_sem.at[1]),
+    ]
+    mine = [
+        pltpu.make_async_copy(
+            patch_ref.at[:, pl.ds(pl.multiple_of(ROWS * mp + 128 * rb, 128), 128)], xin.at[rb, mp], own_sem.at[rb])
+        for rb in range(4)]
+    for copy in loads + mine:
+        copy.start()
+    live = lax.broadcasted_iota(jnp.int32, (TAIL, 1), 0) < inner_ref.shape[0] - MAIN
+    for tail_ref, own, oth in ((inner_tail, w1_own, w1_oth), (outer_tail, w2_own, w2_oth)):
+        value = jnp.where(live, tail_ref[...].astype(F32), 0.0).astype(BF16)
+        own[0:TAIL, :] = value
+        oth[TAIL:2 * TAIL, :] = value
+    sums = tail_refs[0]
+    sums[mp] = jnp.zeros((8, D), F32)
+    for k in range(4):
+        @pl.when(mp == k)
+        def _():
+            sums[k, 2:4, DL * k:DL * k + DL] = text_ref[...].astype(F32)
+    pl.semaphore_wait(barrier, len(everyone))
+
+    def patch_copy(rb, k):
+        who = (mp + k) % 4
+        return pltpu.make_async_remote_copy(
+            src_ref=patch_ref.at[:, pl.ds(pl.multiple_of(ROWS * who + 128 * rb, 128), 128)],
+            dst_ref=xin.at[rb, mp],
+            send_sem=patch_send.at[rb, k - 1], recv_sem=patch_recv.at[rb, k - 1],
+            device_id=(dp, who), device_id_type=MESH)
+
+    def start_patches(rb):
+        for k in range(1, 4):
+            patch_copy(rb, k).start()
+
+    def places(stage):
+        if stage == 0:
+            return [(k, (w1_own, w2_own)[k], (w1_oth, w2_oth)[k],
+                     pl.ds(pl.multiple_of(colour[k] * 16, 16), 16)) for k in range(2)]
+        own, oth = (w1_own, w1_oth) if stage < 5 else (w2_own, w2_oth)
+        base = 128 + 256 * ((stage - 1) % 4)
+        return [(k, own, oth, pl.ds(pl.multiple_of(base + 128 * k + colour[k] * 32, 32), 32)) for k in range(2)]
+
+    def y_copies(stage):
+        return [pltpu.make_async_remote_copy(
+            src_ref=own.at[rows], dst_ref=oth.at[rows],
+            send_sem=y_send.at[stage, k], recv_sem=y_recv.at[stage, k],
+            device_id=peers[LINK[stage, k]], device_id_type=MESH) for k, own, oth, rows in places(stage)]
+
+    def side_copies(stage):
+        copies = []
+        for k, own, oth, rows in places(stage):
+            near = ("xp", "xm") if k == 0 else ("zp", "zm")
+            far = ("zp", "zm") if k == 0 else ("xp", "xm")
+            for j, who in enumerate((near[0], near[1], far[stage % 2])):
+                copies.append(pltpu.make_async_remote_copy(
+                    src_ref=oth.at[rows], dst_ref=oth.at[rows],
+                    send_sem=side_send.at[stage, k, j], recv_sem=side_recv.at[stage, k, j],
+                    device_id=peers[who], device_id_type=MESH))
+        return copies
+
+    def send_y(stage):
+        if stage < STAGES:
+            for copy in y_copies(stage):
+                copy.start()
+
+    def forward(stage):
+        side = side_copies(stage)
+        for k, copy in enumerate(y_copies(stage)):
+            copy.wait_recv()
+            for j in range(3):
+                side[3 * k + j].start()
+        for copy in y_copies(stage):
+            copy.wait_send()
+        send_y(stage + WINDOW)
+
+    def arrive(stage):
+        for copy in side_copies(stage):
+            copy.wait_recv()
+
+    def norm_copy(rb):
+        at = (rb // 2, (rb % 2) * 2 + core)
+        return pltpu.make_async_remote_copy(
+            src_ref=xn.at[at], dst_ref=xn.at[at], send_sem=norm_send.at[rb], recv_sem=norm_recv.at[rb],
+            device_id=peers["core"], device_id_type=MESH)
+
+    def normalise(rb):
+        mine[rb].wait()
+        for k in range(1, 4):
+            patch_copy(rb, k).wait_recv()
+        if rb + 2 < 4:
+            start_patches(rb + 2)
+        raw = xin[rb].reshape(D, 128)
+        wide = raw.astype(F32)
+        wide = wide - jnp.sum(wide, axis=0, keepdims=True) * (1.0 / D)
+        spread = jnp.sum(wide * wide, axis=0, keepdims=True) * (1.0 / D)
+        xn[rb // 2, (rb % 2) * 2 + core] = (wide * lax.rsqrt(spread + epsilon)).astype(BF16).T
+        norm_copy(rb).start()
+        xres[rb] = raw.T
+
+    def expand(half, weights, first, count):
+        block = xn[half].reshape(512, D)
+        for j in range(count):
+            lo = first + 256 * j if first or j else 0
+            hi = first + 256 * (j + 1)
+            hid[half, :, lo:hi] = gelu(lax.dot_general(
+                block, weights[lo:hi, :], (((1,), (1,)), ((), ())), preferred_element_type=F32)).astype(BF16)
+
+    def mix(half, weights, lo, hi, fresh):
+        term = jnp.dot(hid[half, :, lo:hi], weights[lo:hi, :], preferred_element_type=F32).reshape(4, 128, D)
+        acc[half] = term if fresh else acc[half] + term
+
+    def part_copy(rb):
+        return pltpu.make_async_remote_copy(
+            src_ref=part_out.at[rb], dst_ref=part_in.at[rb], send_sem=part_send.at[rb],
+            recv_sem=part_recv.at[rb], device_id=peers["core"], device_id_type=MESH)
+
+    start_patches(0)
+    loads[0].wait()
+    for s in range(WINDOW):
+        send_y(s)
+    start_patches(1)
+    forward(0)
+    normalise(0)
+    forward(1)
+    normalise(1)
+    forward(2)
+    loads[1].wait()
+    for half in range(2):
+        norm_copy(2 * half).wait_recv()
+        norm_copy(2 * half + 1).wait_recv()
+        expand(half, w1_own, 128, 4)
+        forward(3 + 2 * half)
+        mix(half, w2_own, 128, 1152, True)
+        if half == 0:
+            normalise(2)
+            forward(4)
+            normalise(3)
+    for s in range(5):
+        arrive(s)
+
+    def hidden(half, _):
+        block = xn[half].reshape(512, D)
+        for lo, hi in ((0, 128), (128, 384), (384, 640), (640, 896), (896, 1152)):
+            hid[half, :, lo:hi] = gelu(lax.dot_general(
+                block, w1_oth[lo:hi, :], (((1,), (1,)), ((), ())), preferred_element_type=F32)).astype(BF16)
+        return 0
+    hidden(0, 0)
+    forward(6)
+    hidden(1, 0)
+    forward(7)
+    forward(8)
+    arrive(5)
+    arrive(6)
+    mix(0, w2_oth, 0, 640, False)
+    mix(1, w2_oth, 0, 640, False)
+    arrive(7)
+    arrive(8)
+    for half in range(2):
+        mix(half, w2_oth, 640, 1152, False)
+        for r in range(2):
+            rb = half * 2 + r
+            part_out[rb] = acc[half, 2 * r + 1 - core].astype(BF16)
+            part_copy(rb).start()
+
+    n0 = counts_ref[0]
+    n1 = n0 + counts_ref[1]
+
+    def finish(rb, sums):
+        part_copy(rb).wait_recv()
+        value = xres[rb].astype(F32) + (acc[rb // 2, (rb % 2) * 2 + core] + part_in[rb].astype(F32))
+        shifted = value - jnp.sum(value, axis=1, keepdims=True) * (1.0 / D)
+        spread = jnp.sum(shifted * shifted, axis=1, keepdims=True) * (1.0 / D)
+        scale = lax.rsqrt(spread + epsilon)
+        ids = ROWS * mp + 128 * rb + lax.broadcasted_iota(jnp.int32, (128, 1), 0)
+        normed = shifted * scale
+        a = jnp.sum(jnp.where(ids < n0, normed, 0.0), axis=0, keepdims=True)
+        b = jnp.sum(jnp.where((ids >= n0) & (ids < n1), normed, 0.0), axis=0, keepdims=True)
+        return sums[0] + a, sums[1] + b
+    zero = jnp.zeros((1, D), F32)
+    a, b = lax.fori_loop(0, 4, finish, (zero, zero))
+    sums[mp, 0:1, :] = a
+    sums[mp, 1:2, :] = b
+
+    def drain():
+        for rb in range(4):
+            for k in range(1, 4):
+                patch_copy(rb, k).wait_send()
+            norm_copy(rb).wait_send()
+            part_copy(rb).wait_send()
+        for stage in range(STAGES):
+            for copy in side_copies(stage):
+                copy.wait_send()
+    tail_body(counts_ref, pair_ref, scale_ref, bias_ref, loss_ref, emb_ref, txt_ref, *tail_refs, drain)
+
+
+def main_scratch():
+    dma = pltpu.SemaphoreType.DMA
+    return [
+        pltpu.VMEM((D, D), BF16), pltpu.VMEM((D, D), BF16), pltpu.VMEM((D, D), BF16), pltpu.VMEM((D, D), BF16),
+        pltpu.VMEM((4, 4, DL, 128), BF16), pltpu.VMEM((4, 128, D), BF16),
+        pltpu.VMEM((2, 4, 128, D), BF16), pltpu.VMEM((2, 4, 128, D), F32),
+        pltpu.VMEM((2, 512, D), BF16),
+        pltpu.VMEM((4, 128, D), BF16), pltpu.VMEM((4, 128, D), BF16),
+        dma((2,)), dma((4,)), dma((4, 3)), dma((4, 3)), dma((4,)), dma((4,)), dma((STAGES, 2)), dma((STAGES, 2)),
+        dma((STAGES, 2, 3)), dma((STAGES, 2, 3)), dma((4,)), dma((4,)),
+    ]
+
+
+def hand_over(loss_ref, emb_ref, txt_ref, loss_out, emb_out, txt_out):
+    emb_out[...] = emb_ref[...]
+    txt_out[...] = txt_ref[...]
+    loss_out[0] = loss_ref[0, 0]
+    loss_out[1] = loss_ref[1, 0]
 
 
 def shards(
     patches, counts, pair_ids, inner_weight, outer_weight, text_embed, log_scale, logit_bias
 ):
-    group_size = lax.axis_size("mp")
-    shard_rows = patches.shape[0]
-    own_count = shard_rows // group_size
-    row_first = lax.axis_index("mp") * own_count
-    full_rows = lax.all_gather(patches, "mp", axis=1, tiled=True)
-    normed = layer_norm(full_rows.astype(jnp.float32)).astype(jnp.bfloat16)
-    hidden = expand_rows(normed, inner_weight).astype(jnp.bfloat16)
-    mixed_rows = lax.psum_scatter(
-        jnp.dot(hidden, outer_weight, preferred_element_type=jnp.float32),
-        "mp",
-        scatter_dimension=0,
-        tiled=True,
-    )
-    own_rows = lax.dynamic_slice_in_dim(full_rows, row_first, own_count, 0)
-    updated = own_rows.astype(jnp.float32) + mixed_rows
-    final_rows = layer_norm(updated)
-    row_ends = jnp.cumsum(counts)
-    row_starts = row_ends - counts
-    row_ids = row_first + jnp.arange(own_count, dtype=jnp.int32)
-    member = (
-        (row_ids[None, :] >= row_starts[:, None]) & (row_ids[None, :] < row_ends[:, None])
-    ).astype(jnp.float32)
-    partial_value = jnp.dot(member, final_rows, precision=lax.Precision.HIGHEST)
-    return tail(partial_value, text_embed, counts, pair_ids, log_scale, logit_bias)
+    vmem, smem = pl.BlockSpec(memory_space=pltpu.VMEM), pl.BlockSpec(memory_space=pltpu.SMEM)
+    hbm = pl.BlockSpec(memory_space=pl.ANY)
+    end = pl.BlockSpec((TAIL, D), lambda i: (MAIN // TAIL, 0))
+    half = jax.ShapeDtypeStruct((2, DL), F32)
+    inner = inner_weight.T
+    found = pl.pallas_call(
+        main_kernel,
+        grid=(1,),
+        out_shape=(jax.ShapeDtypeStruct((2, 128), F32), half, half),
+        in_specs=[hbm, hbm, hbm, end, end, vmem, smem, smem, smem, smem],
+        out_specs=(vmem, vmem, vmem),
+        scratch_shapes=main_scratch() + tail_scratch(),
+        compiler_params=pltpu.CompilerParams(
+            collective_id=1, has_side_effects=True, vmem_limit_bytes=56 * 2**20),
+        name="tower",
+    )(patches.T, inner, outer_weight, inner, outer_weight, text_embed, counts, pair_ids, log_scale, logit_bias)
+    return pl.pallas_call(
+        hand_over,
+        out_shape=(jax.ShapeDtypeStruct((2,), F32), half, half),
+        in_specs=[vmem, vmem, vmem],
+        out_specs=(smem, vmem, vmem),
+        name="hand_over",
+    )(*found)
 
 
 def solution(mesh):

time: 226 us -> 73.7 us (0.33)
  waiting for transfers between devices: 145 us -> 0 us
  Pallas kernels: 25.4 us -> 71 us
  matrix products: 22 us -> 0 us
  between operations: 15.4 us -> 2.09 us
  local copies, waits for them, and re-layouts: 9.35 us -> 0 us
  other arithmetic: 8.92 us -> 0 us
    reduce_scatter x1 -> x0, waiting for transfers between devices: 84.8 us -> none  [shards(): lax.psum_scatter(jnp.dot(hidden, outer_weight, preferred_element_type=jnp...]
    all_gather x1 -> x0, waiting for transfers between devices: 59.6 us -> none  [shards(): full_rows = lax.all_gather(patches, 'mp', axis=1, tiled=True)]
    pallas_call x1 -> x2, Pallas kernels: 25.4 us -> 71 us  [the longest x1 69.7 us: shards(): pl.pallas_call(main_kernel, grid=(1,), out_shape=(jax.ShapeDtypeStruct((2...]
    dot_general x2 -> x0, matrix products: 22 us -> none  [the longest x1 20.1 us: shards(): jnp.dot(hidden, outer_weight, preferred_element_type=jnp.float32)]
    reduce_sum x4 -> x0, other arithmetic: 8.71 us -> none  [the longest x2 5.65 us: layer_norm(): centre = jnp.mean(values, axis=-1, keepdims=True)]
    unnamed x13 -> x0, local copies, waits for them, and re-layouts: 5.68 us -> none
    dynamic_slice x1 -> x0, local copies, waits for them, and re-layouts: 2.38 us -> none  [shards(): own_rows = lax.dynamic_slice_in_dim(full_rows, row_first, own_count, 0)]
  transfers between devices with their start and end apart: 2 -> 0, of which waited for: 2 -> 0; matrix products, arithmetic and copies ran while one was open for 2% -> 0% of each run, Pallas kernels for 0% -> 0%
where the time goes in v3:
time: 73.7 us; the launch traced here: 73.1 us
  Pallas kernels  71 us (96%)
  between operations  2.09 us (3%)
    pallas_call x1, Pallas kernels, shards(): pl.pallas_call(main_kernel, grid=(1,), out_shape=(jax.ShapeDtypeStruct((2...  69.7 us

profile of v3, /device:TPU:1, one launch (start us, length us, event | category | flops | bytes accessed | tf_op | source)
XLA Modules:
  0.0 73.1 jit_solution(6068613620714971971)
XLA Ops:
  1.9 69.7 %tower.1 = (f32[2,128]{1,0:T(2,128)}, f32[2,288]{1,0:T(2,128)}, f32[2,288]{1,0:T(2,128)}) custom-call(bf16[288,2048]{1,0:T(8,128)(2,1)} %bitcast.4, bf16[1076,1152]{1,0:T(8,128)(2,1)} %bitcast.2, bf16[1076,1152]{1,0:T(8,128)(2,1)} %outer_tail.1, bf16[1076,1152]{1,0:T(8,128)(2,1)} %bitcast.3, bf16[1076,1152]{1,0:T(8,128)(2,1)} %outer_tail.1, ...), custom_call_target="tpu_custom_call" | custom-call | tf_op jit(solution)/shard_map/tower/pallas_call | solution.py:444
  71.6 1.3 %hand_over.1 = (f32[2]{0:T(128)}, f32[2,288]{1,0:T(2,128)}, f32[2,288]{1,0:T(2,128)}) custom-call(f32[2,128]{1,0:T(2,128)} %get-tuple-element.6.loss_ref, f32[2,288]{1,0:T(2,128)} %get-tuple-element.7.emb_ref, f32[2,288]{1,0:T(2,128)} %get-tuple-element.8.txt_ref), custom_call_target="tpu_custom_call" | custom-call | tf_op jit(solution)/shard_map/hand_over/pallas_call | solution.py:455

commit v4 on v0

v4 whole, which is shorter than its diff:
```python
import functools

import jax
import jax.numpy as jnp
from jax import lax
from jax.experimental import pallas as pl
from jax.experimental.pallas import tpu as pltpu
from jax.sharding import PartitionSpec as P

MESH = pl.DeviceIdType.MESH
epsilon = 1e-06
D = 1152
DL = 288
F32, BF16 = jnp.float32, jnp.bfloat16


def coords():
    dp, mp = lax.axis_index("dp"), lax.axis_index("mp")
    return dp // 16, (dp // 2) % 8, dp % 2, mp


def dp_of(x, z, yh):
    return x * 16 + z * 2 + yh


def tail_peers():
    x, z, yh, mp = coords()
    dp = dp_of(x, z, yh)
    group = [(dp, (mp + k) % 4) for k in range(1, 4)]
    line = [(dp_of(x, (z + k) % 8, yh), mp) for k in range(1, 8)]
    plane = [(dp_of((x + k // 2) % 4, z, (yh + k) % 2), mp) for k in range(1, 8)]
    return group, line, plane


def by_parity(column, even, odd):
    return jnp.where(column % 2 == 0, even, odd)


def parity_sums(values):
    own = jnp.sum(values, axis=1, keepdims=True)
    row = lax.broadcasted_iota(jnp.int32, own.shape, 0)
    even = jnp.sum(jnp.where(row % 2 == 0, own, 0.0), axis=0, keepdims=True)
    odd = jnp.sum(jnp.where(row % 2 == 1, own, 0.0), axis=0, keepdims=True)
    return even, odd


def three_terms(values):
    high = values.astype(BF16).astype(F32)
    rest = values - high
    mid = rest.astype(BF16).astype(F32)
    return jnp.concatenate([high, mid, rest - mid], axis=0).astype(BF16)


def stacked(wide):
    return jnp.concatenate([wide[:, 128 * q:128 * q + 128] for q in range(4)], axis=0)


def folded(dots):
    return dots[0:2] + pltpu.roll(dots, 512 - 2, 1)[2:4] + pltpu.roll(dots, 512 - 4, 1)[4:6]


class Tail:
    def __init__(self, text_ref, counts_ref, pair_ref, scale_ref, bias_ref, loss_ref, emb_ref, txt_ref,
                 psum, tss, wide, units, tline, iline, tall, iall, pairs, dots, *sems):
        self.__dict__.update(locals())
        self.x, self.z, self.yh, self.mp = coords()
        self.dp = dp_of(self.x, self.z, self.yh)
        self.own_line = self.x * 2 + self.yh
        self.group, self.line, self.plane = tail_peers()
        self.copies = {}

    def send(self, name, sem, ref, peers):
        sent, got = self.sems[2 * sem], self.sems[2 * sem + 1]
        self.copies[name] = [pltpu.make_async_remote_copy(
            src_ref=ref, dst_ref=ref, send_sem=sent.at[k], recv_sem=got.at[k],
            device_id=peer, device_id_type=MESH) for k, peer in enumerate(peers)]
        for copy in self.copies[name]:
            copy.start()

    def take(self, name):
        for copy in self.copies[name]:
            copy.wait_recv()

    def begin(self):
        text = self.text_ref[...].astype(F32)
        self.tss[self.mp] = jnp.zeros((8, 128), F32)
        self.tss[self.mp, 0:2, :] = jnp.broadcast_to(jnp.sum(text * text, axis=1, keepdims=True), (2, 128))
        self.units[...] = jnp.zeros((4, 8, 128), F32)
        for b in range(3):
            width = 128 if b < 2 else DL - 256
            self.units[0, 2 * b:2 * b + 2, 0:width] = text[:, 128 * b:128 * b + width]
        self.wide[...] = jnp.zeros((8, D + 128), F32)

    def greet(self):
        self.send("tss", 0, self.tss.at[self.mp], self.group)

    def text_line(self):
        self.take("tss")
        total = ((self.tss[0] + self.tss[1]) + self.tss[2]) + self.tss[3]
        norm = lax.rsqrt(total + epsilon)
        row = lax.broadcasted_iota(jnp.int32, (8, 128), 0)
        norm = by_parity(row, norm[0:1], norm[1:2])
        unit = self.units[0] * norm
        self.units[0] = unit
        self.units[1] = norm
        wire = unit.astype(BF16).astype(F32)
        ids = jnp.where(row == 6, self.pair_ref[0], self.pair_ref[1]).astype(F32)
        self.tline[self.z] = jnp.where(row < 6, wire, ids)
        self.send("tline", 1, self.tline.at[self.z], self.line)

    def text_plane(self):
        self.take("tline")
        self.tall[self.own_line] = self.tline[...].reshape(64, 128).astype(BF16)
        self.send("tplane", 2, self.tall.at[self.own_line], self.plane)

    def text_done(self):
        self.take("tplane")
        first = (lax.broadcasted_iota(jnp.int32, (16, 128), 1) == 0).astype(F32).astype(BF16)
        column = lax.dot_general(
            first, self.tall[...].reshape(512, 128), (((1,), (1,)), ((), ())), preferred_element_type=F32)
        self.pairs[...] = pltpu.roll(stacked(column[0:2]), 128 - 4, 1)

    def image_line(self, first, second):
        self.psum[self.mp, 0:1, :] = first
        self.psum[self.mp, 1:2, :] = second
        self.send("psum", 3, self.psum.at[self.mp], self.group)

    def image_rows(self):
        self.take("psum")
        psum, mp = self.psum, self.mp
        row = lax.broadcasted_iota(jnp.int32, (2, 1), 0)
        count = jnp.where(row == 0, self.counts_ref[0], self.counts_ref[1]).astype(F32)
        pooled = (((psum[0] + psum[1]) + psum[2]) + psum[3]) / count
        norm = lax.rsqrt(jnp.sum(pooled * pooled, axis=1, keepdims=True) + epsilon)
        self.wide[0:2, :D] = pooled * norm
        lane = lax.broadcasted_iota(jnp.int32, (2, 128), 1)
        for b in range(3):
            block = self.wide[0:2, 128 * b:128 * b + 128]
            for k in range(1, 4):
                block = jnp.where(mp == k, self.wide[0:2, DL * k + 128 * b:DL * k + 128 * b + 128], block)
            self.units[2, 2 * b:2 * b + 2, :] = block if b < 2 else jnp.where(lane < DL - 256, block, 0.0)
        row8 = lax.broadcasted_iota(jnp.int32, (8, 128), 0)
        unit = self.units[2]
        self.units[3] = by_parity(row8, norm[0:1], norm[1:2]) + jnp.zeros((8, 128), F32)
        wire = unit.astype(BF16).astype(F32)
        self.iline[self.z] = wire
        self.send("iline", 4, self.iline.at[self.z], self.line)

    def left(self, unit):
        wire = unit.astype(BF16).astype(F32)
        return jnp.concatenate([wire, unit - wire], axis=0).astype(BF16)

    def against(self, unit, everyone):
        found = lax.dot_general(
            self.left(unit), everyone, (((1,), (1,)), ((), ())), preferred_element_type=F32)
        return folded(found[0:8]), folded(found[8:16])

    def end(self, meanwhile):
        texts = self.tall[...].reshape(512, 128)
        image, image_rest = self.against(self.units[2], texts)
        self.take("iline")
        self.iall[self.own_line] = self.iline[...].reshape(64, 128).astype(BF16)
        self.send("iplane", 5, self.iall.at[self.own_line], self.plane)
        meanwhile()
        self.take("iplane")
        images = self.iall[...].reshape(512, 128)
        text, text_rest = self.against(self.units[0], images)
        kind = lax.broadcasted_iota(jnp.int32, (2, 512), 1) % 8
        mixed = jnp.where(kind < 2, image, jnp.where(
            kind < 4, pltpu.roll(text, 2, 1), jnp.where(
                kind < 6, pltpu.roll(image_rest, 4, 1), pltpu.roll(text_rest, 6, 1))))
        self.dots[self.mp] = stacked(mixed)
        self.send("dots", 6, self.dots.at[self.mp], self.group)
        row = lax.broadcasted_iota(jnp.int32, (8, 128), 0)
        lane = lax.broadcasted_iota(jnp.int32, (8, 128), 1)
        column = (row // 2) * 128 + lane
        kind = column % 8
        place = column // 64
        shard = (place // 2) * 16 + ((column // 8) % 8) * 2 + place % 2
        other = shard * 2 + kind % 2
        own = row % 2
        own_pair = by_parity(row, self.pair_ref[0], self.pair_ref[1])
        match = jnp.where(kind < 2, own_pair, self.pairs[...].astype(jnp.int32)) == jnp.where(
            kind < 2, other, self.dp * 2 + own)
        label = jnp.where(match, 1.0, -1.0)
        scale = jnp.exp(jnp.full((8, 128), self.scale_ref[0], F32))
        self.take("dots")
        dots = self.dots
        dot = ((dots[0] + dots[1]) + dots[2]) + dots[3]
        turned = -label * (scale * dot + self.bias_ref[0])
        small = jnp.exp(-jnp.abs(turned))
        soft = jnp.where(kind < 2, jnp.maximum(turned, 0.0) + jnp.log1p(small), 0.0)
        sigmoid = jnp.where(turned >= 0, 1.0, small) / (1.0 + small)
        slope = jnp.where(kind < 4, -label * sigmoid, 0.0)
        term = scale * slope * (dot + pltpu.roll(dot, 128 - 4, 1))
        loss = parity_sums(soft)
        image_proj = parity_sums(jnp.where(kind < 2, term, 0.0))
        text_proj = parity_sums(jnp.where(kind >= 2, term, 0.0))
        blank = jnp.zeros((2, 512), F32)
        for everyone, kept, proj, at, out in (
            (texts, kind < 2, image_proj, 2, self.emb_ref), (images, kind >= 2, text_proj, 0, self.txt_ref)
        ):
            flat = jnp.where(kept, slope, 0.0)
            flat = jnp.concatenate([flat[2 * q:2 * q + 2] for q in range(4)], axis=1)
            if at == 0:
                flat = pltpu.roll(flat, 512 - 2, 1)
            spread = jnp.concatenate([flat, pltpu.roll(flat, 2, 1), pltpu.roll(flat, 4, 1), blank], axis=0)
            found = jnp.dot(three_terms(spread), everyone, preferred_element_type=F32)
            direction = (found[0:8] + (found[8:16] + found[16:24])) * scale
            grad = (direction - self.units[at] * by_parity(row, proj[0], proj[1])) * self.units[at + 1]
            for b in range(3):
                width = 128 if b < 2 else DL - 256
                out[:, 128 * b:128 * b + width] = grad[2 * b:2 * b + 2, 0:width]
        self.loss_ref[...] = by_parity(lax.broadcasted_iota(jnp.int32, (2, 128), 0), loss[0], loss[1])
        for copies in self.copies.values():
            for copy in copies:
                copy.wait_send()


def tail_scratch():
    dma = pltpu.SemaphoreType.DMA
    pair = lambda n: [dma((n,)), dma((n,))]
    return [
        pltpu.VMEM((4, 2, D), F32), pltpu.VMEM((4, 8, 128), F32), pltpu.VMEM((8, D + 128), F32),
        pltpu.VMEM((4, 8, 128), F32), pltpu.VMEM((8, 8, 128), F32), pltpu.VMEM((8, 8, 128), F32),
        pltpu.VMEM((8, 64, 128), BF16), pltpu.VMEM((8, 64, 128), BF16), pltpu.VMEM((8, 128), F32),
        pltpu.VMEM((4, 8, 128), F32),
    ] + pair(3) + pair(7) + pair(7) + pair(3) + pair(7) + pair(7) + pair(3)


ROWS = 512
MAIN = 1024
TAIL = 64
WINDOW = 4
STAGES = 9
HI = [(0, 0), (0, 1), (1, 0), (1, 1), (2, 0), (2, 1), (3, 1), (4, 0), (5, 1), (6, 0), (6, 1), (7, 1)]
LO = [('P', 0), ('P', 1), (3, 0), ('P', 2), (4, 1), ('P', 3), (5, 0), (7, 0), (8, 0), (8, 1)]
ORDER = [('F', 0, 0), ('F', 0, 1), ('N', 0), ('F', 1, 0), ('F', 1, 1), ('N', 1), ('F', 2, 0), ('F', 3, 0), ('F', 2, 1), ('E', 0, 0), ('E', 0, 1), ('E', 0, 2), ('E', 0, 3), ('F', 3, 1), ('M', 0, 0), ('N', 2), ('F', 4, 0), ('M', 0, 1), ('F', 4, 1), ('H', 0, 0), ('F', 5, 1), ('H', 0, 1), ('H', 0, 2), ('H', 0, 3), ('F', 6, 0), ('N', 3), ('F', 6, 1), ('H', 0, 4), ('F', 5, 0), ('F', 7, 1), ('E', 1, 0), ('E', 1, 1), ('E', 1, 2), ('F', 7, 0), ('E', 1, 3), ('M', 1, 0), ('F', 8, 0), ('M', 1, 1), ('H', 1, 0), ('H', 1, 1), ('F', 8, 1), ('H', 1, 2), ('H', 1, 3), ('H', 1, 4), ('A', 0, 0), ('A', 0, 1), ('A', 1, 0), ('A', 1, 1), ('B', 0), ('B', 1)]


def main_peers():
    x, z, yh, mp = coords()
    dp = dp_of(x, z, yh)
    return dict(
        core=(dp, mp + 1 - 2 * (mp % 2)),
        lo=(dp, (mp + 2) % 4),
        cross=(dp, 3 - mp),
        hi=(dp + 1 - 2 * (dp % 2), (mp + 2) % 4),
        xp=(dp_of((x + 1) % 4, z, yh), mp),
        xm=(dp_of((x + 3) % 4, z, yh), mp),
        zp=(dp_of(x, (z + 1) % 8, yh), mp),
        zm=(dp_of(x, (z + 7) % 8, yh), mp),
    )


def gelu(u):
    inner = u * (0.7978845608028654 + 0.035677408136300125 * (u * u))
    half = 0.5 * u
    return half + half * jnp.tanh(inner)


def main_kernel(
    patch_ref, inner_ref, outer_ref, inner_tail, outer_tail, text_ref, counts_ref, pair_ref, scale_ref, bias_ref,
    loss_ref, emb_ref, txt_ref,
    w1_own, w2_own, w1_oth, w2_oth, xin, xres, xn, acc, hid, part_out, part_in,
    load_sem, own_sem, patch_send, patch_recv, norm_send, norm_recv, y_send, y_recv,
    side_send, side_recv, part_send, part_recv, *tail_refs,
):
    x, z, yh, mp = coords()
    dp = dp_of(x, z, yh)
    core = mp % 2
    colour = [(x + 2 * z) % 4, (2 * x + z) % 4]
    peers = main_peers()
    barrier = pltpu.get_barrier_semaphore()
    group, line, plane = tail_peers()
    everyone = [peers["hi"]] + group + line + plane
    for peer in everyone:
        pl.semaphore_signal(barrier, inc=1, device_id=peer, device_id_type=MESH)
    mains = pl.ds(2 * TAIL, MAIN)
    loads = [
        pltpu.make_async_copy(inner_ref.at[pl.ds(0, MAIN)], w1_own.at[mains], load_sem.at[0]),
        pltpu.make_async_copy(outer_ref.at[pl.ds(0, MAIN)], w2_own.at[mains], load_sem.at[1]),
    ]
    mine = [
        pltpu.make_async_copy(
            patch_ref.at[:, pl.ds(pl.multiple_of(ROWS * mp + 128 * rb, 128), 128)], xin.at[rb, mp], own_sem.at[rb])
        for rb in range(4)]
    for copy in mine + loads:
        copy.start()
    live = lax.broadcasted_iota(jnp.int32, (TAIL, 1), 0) < inner_ref.shape[0] - MAIN
    for tail_ref, own, oth in ((inner_tail, w1_own, w1_oth), (outer_tail, w2_own, w2_oth)):
        value = jnp.where(live, tail_ref[...].astype(F32), 0.0).astype(BF16)
        own[0:TAIL, :] = value
        oth[TAIL:2 * TAIL, :] = value
    tail = Tail(text_ref, counts_ref, pair_ref, scale_ref, bias_ref, loss_ref, emb_ref, txt_ref, *tail_refs)
    tail.begin()
    pl.semaphore_wait(barrier, len(everyone))

    def patch_copies(rb):
        return [pltpu.make_async_remote_copy(
            src_ref=patch_ref.at[:, pl.ds(pl.multiple_of(ROWS * ((mp + k) % 4) + 128 * rb, 128), 128)],
            dst_ref=xin.at[rb, mp],
            send_sem=patch_send.at[rb, k - 1], recv_sem=patch_recv.at[rb, k - 1],
            device_id=(dp, (mp + k) % 4), device_id_type=MESH) for k in range(1, 4)]

    def place(stage, k):
        if stage == 0:
            rows = pl.ds(pl.multiple_of(colour[k] * 16, 16), 16)
            return (w1_own, w2_own)[k].at[rows], (w1_oth, w2_oth)[k].at[rows]
        src, dst = (inner_ref, w1_oth) if stage < 5 else (outer_ref, w2_oth)
        first = 256 * ((stage - 1) % 4) + 128 * k + colour[k] * 32
        return src.at[pl.ds(pl.multiple_of(first, 32), 32)], dst.at[pl.ds(pl.multiple_of(first + 128, 32), 32)]

    def y_copy(stage, k):
        src, dst = place(stage, k)
        return pltpu.make_async_remote_copy(
            src_ref=src, dst_ref=dst, send_sem=y_send.at[stage, k], recv_sem=y_recv.at[stage, k],
            device_id=peers["hi" if (stage, k) in HI else "lo"], device_id_type=MESH)

    def side_copies(stage, k):
        near, far = (("xp", "xm"), ("zp", "zm")) if k == 0 else (("zp", "zm"), ("xp", "xm"))
        _, at = place(stage, k)
        return [pltpu.make_async_remote_copy(
            src_ref=at, dst_ref=at, send_sem=side_send.at[stage, k, j], recv_sem=side_recv.at[stage, k, j],
            device_id=peers[who], device_id_type=MESH) for j, who in enumerate((near[0], near[1], far[stage % 2]))]

    queues = {"hi": list(HI), "lo": list(LO)}

    def issue(link):
        if queues[link]:
            item = queues[link].pop(0)
            for copy in patch_copies(item[1]) if item[0] == "P" else [y_copy(*item)]:
                copy.start()

    def forward(stage, k):
        copy = y_copy(stage, k)
        copy.wait_recv()
        for side in side_copies(stage, k):
            side.start()
        copy.wait_send()
        issue("hi" if (stage, k) in HI else "lo")

    arrived = set()

    def arrive(stage):
        if stage not in arrived:
            arrived.add(stage)
            for k in range(2):
                for copy in side_copies(stage, k):
                    copy.wait_recv()

    def norm_copy(rb):
        at = (rb // 2, (rb % 2) * 2 + core)
        return pltpu.make_async_remote_copy(
            src_ref=xn.at[at], dst_ref=xn.at[at], send_sem=norm_send.at[rb], recv_sem=norm_recv.at[rb],
            device_id=peers["core"], device_id_type=MESH)

    def normalise(rb):
        mine[rb].wait()
        for copy in patch_copies(rb):
            copy.wait_recv()
        issue("lo")
        raw = xin[rb].reshape(D, 128)
        wide = raw.astype(F32)
        wide = wide - jnp.sum(wide, axis=0, keepdims=True) * (1.0 / D)
        spread = jnp.sum(wide * wide, axis=0, keepdims=True) * (1.0 / D)
        xn[rb // 2, (rb % 2) * 2 + core] = (wide * lax.rsqrt(spread + epsilon)).astype(BF16).T
        norm_copy(rb).start()
        xres[rb] = raw.T

    def expand(half, weights, lo, hi):
        hid[half, :, lo:hi] = gelu(lax.dot_general(
            xn[half].reshape(512, D), weights[lo:hi, :], (((1,), (1,)), ((), ())), preferred_element_type=F32)).astype(BF16)

    def own_expand(half, j):
        if j == 0:
            norm_copy(2 * half).wait_recv()
            norm_copy(2 * half + 1).wait_recv()
            if half == 0:
                loads[0].wait()
        expand(half, w1_own, 128 + 256 * j, 384 + 256 * j)

    def mix(half, weights, lo, hi, left, right, fresh):
        term = jnp.dot(
            hid[half, :, lo:hi], weights[lo:hi, left:right], preferred_element_type=F32).reshape(4, 128, right - left)
        acc[half, :, :, left:right] = term if fresh else acc[half, :, :, left:right] + term

    def own_mix(half, n):
        if half == 0 and n == 0:
            loads[1].wait()
        mix(half, w2_own, 128, 1152, (0, 640)[n], (640, 1152)[n], True)

    def other_expand(half, j):
        arrive(j)
        expand(half, w1_oth, 256 * j - 128 if j else 0, 256 * j + 128)

    def other_mix(half, n):
        arrive(5)
        arrive(6)
        mix(half, w2_oth, 0, 640, (0, 640)[n], (640, 1152)[n], False)

    def part_copy(rb):
        return pltpu.make_async_remote_copy(
            src_ref=part_out.at[rb], dst_ref=part_in.at[rb], send_sem=part_send.at[rb],
            recv_sem=part_recv.at[rb], device_id=peers["core"], device_id_type=MESH)

    def last_mix(half):
        arrive(7)
        arrive(8)
        mix(half, w2_oth, 640, 1152, 0, D, False)
        for r in range(2):
            rb = half * 2 + r
            part_out[rb] = acc[half, 2 * r + 1 - core].astype(BF16)
            part_copy(rb).start()

    tail.greet()
    for _ in range(WINDOW):
        issue("hi")
        issue("lo")
    steps = dict(
        F=forward, N=normalise, E=own_expand, M=own_mix, H=other_expand, A=other_mix, B=last_mix)
    texts = {2: tail.text_line, 20: tail.text_plane, 46: tail.text_done}
    for at, (name, *where) in enumerate(ORDER):
        steps[name](*where)
        if at in texts:
            texts[at]()

    n0 = counts_ref[0]
    n1 = n0 + counts_ref[1]

    def finish(rb, totals):
        part_copy(rb).wait_recv()
        value = xres[rb].astype(F32) + (acc[rb // 2, (rb % 2) * 2 + core] + part_in[rb].astype(F32))
        shifted = value - jnp.sum(value, axis=1, keepdims=True) * (1.0 / D)
        spread = jnp.sum(shifted * shifted, axis=1, keepdims=True) * (1.0 / D)
        scale = lax.rsqrt(spread + epsilon)
        ids = ROWS * mp + 128 * rb + lax.broadcasted_iota(jnp.int32, (128, 1), 0)
        normed = shifted * scale
        a = jnp.sum(jnp.where(ids < n0, normed, 0.0), axis=0, keepdims=True)
        b = jnp.sum(jnp.where((ids >= n0) & (ids < n1), normed, 0.0), axis=0, keepdims=True)
        return totals[0] + a, totals[1] + b
    zero = jnp.zeros((1, D), F32)
    a, b = lax.fori_loop(0, 4, finish, (zero, zero))
    tail.image_line(a, b)
    tail.image_rows()

    def drain():
        for rb in range(4):
            for copy in patch_copies(rb):
                copy.wait_send()
            norm_copy(rb).wait_send()
            part_copy(rb).wait_send()
        for stage in range(STAGES):
            for k in range(2):
                for copy in side_copies(stage, k):
                    copy.wait_send()
    tail.end(drain)


def main_scratch():
    dma = pltpu.SemaphoreType.DMA
    return [
        pltpu.VMEM((D, D), BF16), pltpu.VMEM((D, D), BF16), pltpu.VMEM((D, D), BF16), pltpu.VMEM((D, D), BF16),
        pltpu.VMEM((4, 4, DL, 128), BF16), pltpu.VMEM((4, 128, D), BF16),
        pltpu.VMEM((2, 4, 128, D), BF16), pltpu.VMEM((2, 4, 128, D), F32),
        pltpu.VMEM((2, 512, D), BF16),
        pltpu.VMEM((4, 128, D), BF16), pltpu.VMEM((4, 128, D), BF16),
        dma((2,)), dma((4,)), dma((4, 3)), dma((4, 3)), dma((4,)), dma((4,)), dma((STAGES, 2)), dma((STAGES, 2)),
        dma((STAGES, 2, 3)), dma((STAGES, 2, 3)), dma((4,)), dma((4,)),
    ]


def hand_over(loss_ref, emb_ref, txt_ref, loss_out, emb_out, txt_out):
    emb_out[...] = emb_ref[...]
    txt_out[...] = txt_ref[...]
    loss_out[0] = loss_ref[0, 0]
    loss_out[1] = loss_ref[1, 0]


def shards(
    patches, counts, pair_ids, inner_weight, outer_weight, text_embed, log_scale, logit_bias
):
    vmem, smem = pl.BlockSpec(memory_space=pltpu.VMEM), pl.BlockSpec(memory_space=pltpu.SMEM)
    hbm = pl.BlockSpec(memory_space=pl.ANY)
    end = pl.BlockSpec((TAIL, D), lambda i: (MAIN // TAIL, 0))
    half = jax.ShapeDtypeStruct((2, DL), F32)
    inner = inner_weight.T
    found = pl.pallas_call(
        main_kernel,
        grid=(1,),
        out_shape=(jax.ShapeDtypeStruct((2, 128), F32), half, half),
        in_specs=[hbm, hbm, hbm, end, end, vmem, smem, smem, smem, smem],
        out_specs=(vmem, vmem, vmem),
        scratch_shapes=main_scratch() + tail_scratch(),
        compiler_params=pltpu.CompilerParams(
            collective_id=1, has_side_effects=True, vmem_limit_bytes=56 * 2**20),
        name="tower",
    )(patches.T, inner, outer_weight, inner, outer_weight, text_embed, counts, pair_ids, log_scale, logit_bias)
    return pl.pallas_call(
        hand_over,
        out_shape=(jax.ShapeDtypeStruct((2,), F32), half, half),
        in_specs=[vmem, vmem, vmem],
        out_specs=(smem, vmem, vmem),
        name="hand_over",
    )(*found)


def solution(mesh):
    placed = (
        P("dp", "mp"),
        P("dp"),
        P("dp"),
        P(None, "mp"),
        P("mp", None),
        P("dp", "mp"),
        P(),
        P(),
    )
    return jax.shard_map(
        shards,
        mesh=mesh,
        in_specs=placed,
        out_specs=(P("dp"), P("dp", "mp"), P("dp", "mp")),
        check_vma=False,
    )
```

time: 948 us -> 69.4 us (0.07)
  the two profiles are of different devices: /device:TPU:32 before, /device:TPU:1 now
where the time goes in v4:
time: 69.4 us; the launch traced here: 69.2 us
  Pallas kernels  67.1 us (97%)
  between operations  2.09 us (3%)
    pallas_call x1, Pallas kernels, shards(): pl.pallas_call(main_kernel, grid=(1,), out_shape=(jax.ShapeDtypeStruct((2...  65.8 us

profile of v4, /device:TPU:1, one launch (start us, length us, event | category | flops | bytes accessed | tf_op | source)
XLA Modules:
  0.0 69.2 jit_solution(3709488112471686038)
XLA Ops:
  1.9 65.8 %tower.1 = (f32[2,128]{1,0:T(2,128)}, f32[2,288]{1,0:T(2,128)}, f32[2,288]{1,0:T(2,128)}) custom-call(bf16[288,2048]{1,0:T(8,128)(2,1)} %bitcast.4, bf16[1076,1152]{1,0:T(8,128)(2,1)} %bitcast.2, bf16[1076,1152]{1,0:T(8,128)(2,1)} %outer_tail.1, bf16[1076,1152]{1,0:T(8,128)(2,1)} %bitcast.3, bf16[1076,1152]{1,0:T(8,128)(2,1)} %outer_tail.1, ...), custom_call_target="tpu_custom_call" | custom-call | tf_op jit(solution)/shard_map/tower/pallas_call | solution.py:488
  67.8 1.3 %hand_over.1 = (f32[2]{0:T(128)}, f32[2,288]{1,0:T(2,128)}, f32[2,288]{1,0:T(2,128)}) custom-call(f32[2,128]{1,0:T(2,128)} %get-tuple-element.6.loss_ref, f32[2,288]{1,0:T(2,128)} %get-tuple-element.7.emb_ref, f32[2,288]{1,0:T(2,128)} %get-tuple-element.8.txt_ref), custom_call_target="tpu_custom_call" | custom-call | tf_op jit(solution)/shard_map/hand_over/pallas_call | solution.py:499

commit v5 on v4

--- a/solution.py
+++ b/solution.py
@@ -231,11 +231,12 @@
 ROWS = 512
 MAIN = 1024
 TAIL = 64
-WINDOW = 4
+UNITS = 1076
+WINDOW = 6
 STAGES = 9
-HI = [(0, 0), (0, 1), (1, 0), (1, 1), (2, 0), (2, 1), (3, 1), (4, 0), (5, 1), (6, 0), (6, 1), (7, 1)]
-LO = [('P', 0), ('P', 1), (3, 0), ('P', 2), (4, 1), ('P', 3), (5, 0), (7, 0), (8, 0), (8, 1)]
-ORDER = [('F', 0, 0), ('F', 0, 1), ('N', 0), ('F', 1, 0), ('F', 1, 1), ('N', 1), ('F', 2, 0), ('F', 3, 0), ('F', 2, 1), ('E', 0, 0), ('E', 0, 1), ('E', 0, 2), ('E', 0, 3), ('F', 3, 1), ('M', 0, 0), ('N', 2), ('F', 4, 0), ('M', 0, 1), ('F', 4, 1), ('H', 0, 0), ('F', 5, 1), ('H', 0, 1), ('H', 0, 2), ('H', 0, 3), ('F', 6, 0), ('N', 3), ('F', 6, 1), ('H', 0, 4), ('F', 5, 0), ('F', 7, 1), ('E', 1, 0), ('E', 1, 1), ('E', 1, 2), ('F', 7, 0), ('E', 1, 3), ('M', 1, 0), ('F', 8, 0), ('M', 1, 1), ('H', 1, 0), ('H', 1, 1), ('F', 8, 1), ('H', 1, 2), ('H', 1, 3), ('H', 1, 4), ('A', 0, 0), ('A', 0, 1), ('A', 1, 0), ('A', 1, 1), ('B', 0), ('B', 1)]
+HI = [(1, 0), (2, 0), (2, 1), (0, 0), (0, 1), (3, 0), (3, 1), (4, 1), (5, 1), (6, 0), (6, 1), (8, 0)]
+LO = [('P', 0), ('P', 1), (1, 1), ('P', 2), (4, 0), ('P', 3), (5, 0), (7, 0), (7, 1), (8, 1)]
+ORDER = [('F', 1, 0), ('F', 2, 0), ('N', 0), ('F', 2, 1), ('e', 0, 0), ('F', 0, 0), ('e', 0, 1), ('F', 0, 1), ('N', 1), ('m', 0), ('F', 3, 0), ('F', 1, 1), ('e', 1, 0), ('e', 1, 1), ('F', 3, 1), ('m', 1), ('H', 0, 0), ('H', 0, 2), ('F', 4, 1), ('N', 2), ('F', 4, 0), ('F', 5, 1), ('H', 0, 1), ('F', 6, 0), ('H', 0, 3), ('F', 6, 1), ('N', 3), ('H', 0, 4), ('F', 5, 0), ('F', 8, 0), ('E', 1, 0), ('E', 1, 1), ('E', 1, 2), ('F', 7, 0), ('E', 1, 3), ('M', 1, 0), ('F', 7, 1), ('M', 1, 1), ('H', 1, 0), ('H', 1, 1), ('F', 8, 1), ('H', 1, 2), ('H', 1, 3), ('H', 1, 4), ('A', 0, 0), ('A', 0, 1), ('A', 1, 0), ('A', 1, 1), ('B', 0), ('B', 1)]
 
 
 def main_peers():
@@ -260,11 +261,11 @@
 
 
 def main_kernel(
-    patch_ref, inner_ref, outer_ref, inner_tail, outer_tail, text_ref, counts_ref, pair_ref, scale_ref, bias_ref,
+    patch_ref, inner_ref, outer_ref, text_ref, counts_ref, pair_ref, scale_ref, bias_ref,
     loss_ref, emb_ref, txt_ref,
-    w1_own, w2_own, w1_oth, w2_oth, xin, xres, xn, acc, hid, part_out, part_in,
+    w1_own, w2_own, tails, w1_oth, w2_oth, xin, xres, xn, acc, hid, part_out, part_in,
     load_sem, own_sem, patch_send, patch_recv, norm_send, norm_recv, y_send, y_recv,
-    side_send, side_recv, part_send, part_recv, *tail_refs,
+    side_send, side_recv, part_send, part_recv, heard, *tail_refs,
 ):
     x, z, yh, mp = coords()
     dp = dp_of(x, z, yh)
@@ -272,14 +273,11 @@
     colour = [(x + 2 * z) % 4, (2 * x + z) % 4]
     peers = main_peers()
     barrier = pltpu.get_barrier_semaphore()
-    group, line, plane = tail_peers()
-    everyone = [peers["hi"]] + group + line + plane
-    for peer in everyone:
+    for peer in peers.values():
         pl.semaphore_signal(barrier, inc=1, device_id=peer, device_id_type=MESH)
-    mains = pl.ds(2 * TAIL, MAIN)
     loads = [
-        pltpu.make_async_copy(inner_ref.at[pl.ds(0, MAIN)], w1_own.at[mains], load_sem.at[0]),
-        pltpu.make_async_copy(outer_ref.at[pl.ds(0, MAIN)], w2_own.at[mains], load_sem.at[1]),
+        pltpu.make_async_copy(inner_ref, w1_own, load_sem.at[0]),
+        pltpu.make_async_copy(outer_ref, w2_own, load_sem.at[1]),
     ]
     mine = [
         pltpu.make_async_copy(
@@ -287,14 +285,9 @@
         for rb in range(4)]
     for copy in mine + loads:
         copy.start()
-    live = lax.broadcasted_iota(jnp.int32, (TAIL, 1), 0) < inner_ref.shape[0] - MAIN
-    for tail_ref, own, oth in ((inner_tail, w1_own, w1_oth), (outer_tail, w2_own, w2_oth)):
-        value = jnp.where(live, tail_ref[...].astype(F32), 0.0).astype(BF16)
-        own[0:TAIL, :] = value
-        oth[TAIL:2 * TAIL, :] = value
     tail = Tail(text_ref, counts_ref, pair_ref, scale_ref, bias_ref, loss_ref, emb_ref, txt_ref, *tail_refs)
     tail.begin()
-    pl.semaphore_wait(barrier, len(everyone))
+    pl.semaphore_wait(barrier, len(peers))
 
     def patch_copies(rb):
         return [pltpu.make_async_remote_copy(
@@ -306,7 +299,7 @@
     def place(stage, k):
         if stage == 0:
             rows = pl.ds(pl.multiple_of(colour[k] * 16, 16), 16)
-            return (w1_own, w2_own)[k].at[rows], (w1_oth, w2_oth)[k].at[rows]
+            return tails.at[k, rows], (w1_oth, w2_oth)[k].at[rows]
         src, dst = (inner_ref, w1_oth) if stage < 5 else (outer_ref, w2_oth)
         first = 256 * ((stage - 1) % 4) + 128 * k + colour[k] * 32
         return src.at[pl.ds(pl.multiple_of(first, 32), 32)], dst.at[pl.ds(pl.multiple_of(first + 128, 32), 32)]
@@ -337,7 +330,6 @@
         copy.wait_recv()
         for side in side_copies(stage, k):
             side.start()
-        copy.wait_send()
         issue("hi" if (stage, k) in HI else "lo")
 
     arrived = set()
@@ -368,36 +360,46 @@
         norm_copy(rb).start()
         xres[rb] = raw.T
 
-    def expand(half, weights, lo, hi):
-        hid[half, :, lo:hi] = gelu(lax.dot_general(
-            xn[half].reshape(512, D), weights[lo:hi, :], (((1,), (1,)), ((), ())), preferred_element_type=F32)).astype(BF16)
+    def expand(rows, weights, lo, hi):
+        return gelu(lax.dot_general(
+            rows, weights[lo:hi, :], (((1,), (1,)), ((), ())), preferred_element_type=F32)).astype(BF16)
+
+    def quarter_expand(rb, n):
+        if n == 0:
+            norm_copy(rb).wait_recv()
+        for j in (2 * n, 2 * n + 1):
+            hid[0, 256 * rb:256 * rb + 256, 128 + 256 * j:384 + 256 * j] = expand(
+                xn[0, 2 * rb:2 * rb + 2].reshape(256, D), w1_own, 256 * j, 256 * j + 256)
+
+    def quarter_mix(rb):
+        acc[0, 2 * rb:2 * rb + 2] = jnp.dot(
+            hid[0, 256 * rb:256 * rb + 256, 128:1152], w2_own[0:MAIN, :], preferred_element_type=F32).reshape(2, 128, D)
 
     def own_expand(half, j):
         if j == 0:
             norm_copy(2 * half).wait_recv()
             norm_copy(2 * half + 1).wait_recv()
-            if half == 0:
-                loads[0].wait()
-        expand(half, w1_own, 128 + 256 * j, 384 + 256 * j)
-
-    def mix(half, weights, lo, hi, left, right, fresh):
-        term = jnp.dot(
-            hid[half, :, lo:hi], weights[lo:hi, left:right], preferred_element_type=F32).reshape(4, 128, right - left)
-        acc[half, :, :, left:right] = term if fresh else acc[half, :, :, left:right] + term
+        hid[half, :, 128 + 256 * j:384 + 256 * j] = expand(
+            xn[half].reshape(512, D), w1_own, 256 * j, 256 * j + 256)
+
+    def mix(half, weights, lo, hi, left, right):
+        return jnp.dot(
+            hid[half, :, lo:hi], weights[:, left:right], preferred_element_type=F32).reshape(4, 128, right - left)
 
     def own_mix(half, n):
-        if half == 0 and n == 0:
-            loads[1].wait()
-        mix(half, w2_own, 128, 1152, (0, 640)[n], (640, 1152)[n], True)
+        left, right = ((0, 640), (640, 1152))[n]
+        acc[half, :, :, left:right] = mix(half, w2_own.at[0:MAIN], 128, 1152, left, right)
 
     def other_expand(half, j):
         arrive(j)
-        expand(half, w1_oth, 256 * j - 128 if j else 0, 256 * j + 128)
+        lo, hi = 256 * j - 128 if j else 0, 256 * j + 128
+        hid[half, :, lo:hi] = expand(xn[half].reshape(512, D), w1_oth, lo, hi)
 
     def other_mix(half, n):
         arrive(5)
         arrive(6)
-        mix(half, w2_oth, 0, 640, (0, 640)[n], (640, 1152)[n], False)
+        left, right = ((0, 640), (640, 1152))[n]
+        acc[half, :, :, left:right] += mix(half, w2_oth.at[0:640], 0, 640, left, right)
 
     def part_copy(rb):
         return pltpu.make_async_remote_copy(
@@ -407,19 +409,43 @@
     def last_mix(half):
         arrive(7)
         arrive(8)
-        mix(half, w2_oth, 640, 1152, 0, D, False)
+        acc[half] += mix(half, w2_oth.at[640:1152], 640, 1152, 0, D)
         for r in range(2):
             rb = half * 2 + r
             part_out[rb] = acc[half, 2 * r + 1 - core].astype(BF16)
             part_copy(rb).start()
 
     tail.greet()
-    for _ in range(WINDOW):
+    for _ in range(2):
+        issue("hi")
+        issue("lo")
+    kept = inner_ref.shape[0] - MAIN
+    for k, (own, oth) in enumerate(((w1_own, w1_oth), (w2_own, w2_oth))):
+        loads[k].wait()
+        value, blank = own[MAIN:MAIN + kept, :], jnp.zeros((TAIL - kept, D), BF16)
+        tails[k, 0:kept, :] = value
+        tails[k, kept:TAIL, :] = blank
+        oth[TAIL:TAIL + kept, :] = value
+        oth[TAIL + kept:2 * TAIL, :] = blank
+    for _ in range(WINDOW - 2):
         issue("hi")
         issue("lo")
     steps = dict(
-        F=forward, N=normalise, E=own_expand, M=own_mix, H=other_expand, A=other_mix, B=last_mix)
-    texts = {2: tail.text_line, 20: tail.text_plane, 46: tail.text_done}
+        F=forward, N=normalise, e=quarter_expand, m=quarter_mix, E=own_expand, M=own_mix, H=other_expand, A=other_mix, B=last_mix)
+
+    beside = [peers[name] for name in ("lo", "hi", "xp", "xm", "zp", "zm")]
+
+    def tell(n):
+        for peer in beside:
+            pl.semaphore_signal(heard.at[n], inc=1, device_id=peer, device_id_type=MESH)
+
+    def hear(n):
+        pl.semaphore_wait(heard.at[n], len(beside))
+        if n < 2:
+            tell(n + 1)
+    tell(0)
+    texts = {4: lambda: hear(0), 8: lambda: hear(1), 12: lambda: (hear(2), tail.text_line()),
+             26: tail.text_plane, 48: tail.text_done}
     for at, (name, *where) in enumerate(ORDER):
         steps[name](*where)
         if at in texts:
@@ -452,7 +478,7 @@
             part_copy(rb).wait_send()
         for stage in range(STAGES):
             for k in range(2):
-                for copy in side_copies(stage, k):
+                for copy in [y_copy(stage, k)] + side_copies(stage, k):
                     copy.wait_send()
     tail.end(drain)
 
@@ -460,13 +486,14 @@
 def main_scratch():
     dma = pltpu.SemaphoreType.DMA
     return [
-        pltpu.VMEM((D, D), BF16), pltpu.VMEM((D, D), BF16), pltpu.VMEM((D, D), BF16), pltpu.VMEM((D, D), BF16),
+        pltpu.VMEM((UNITS, D), BF16), pltpu.VMEM((UNITS, D), BF16), pltpu.VMEM((2, TAIL, D), BF16),
+        pltpu.VMEM((D, D), BF16), pltpu.VMEM((D, D), BF16),
         pltpu.VMEM((4, 4, DL, 128), BF16), pltpu.VMEM((4, 128, D), BF16),
         pltpu.VMEM((2, 4, 128, D), BF16), pltpu.VMEM((2, 4, 128, D), F32),
         pltpu.VMEM((2, 512, D), BF16),
         pltpu.VMEM((4, 128, D), BF16), pltpu.VMEM((4, 128, D), BF16),
         dma((2,)), dma((4,)), dma((4, 3)), dma((4, 3)), dma((4,)), dma((4,)), dma((STAGES, 2)), dma((STAGES, 2)),
-        dma((STAGES, 2, 3)), dma((STAGES, 2, 3)), dma((4,)), dma((4,)),
+        dma((STAGES, 2, 3)), dma((STAGES, 2, 3)), dma((4,)), dma((4,)), pltpu.SemaphoreType.REGULAR((3,)),
     ]
 
 
@@ -482,20 +509,17 @@
 ):
     vmem, smem = pl.BlockSpec(memory_space=pltpu.VMEM), pl.BlockSpec(memory_space=pltpu.SMEM)
     hbm = pl.BlockSpec(memory_space=pl.ANY)
-    end = pl.BlockSpec((TAIL, D), lambda i: (MAIN // TAIL, 0))
     half = jax.ShapeDtypeStruct((2, DL), F32)
-    inner = inner_weight.T
     found = pl.pallas_call(
         main_kernel,
-        grid=(1,),
         out_shape=(jax.ShapeDtypeStruct((2, 128), F32), half, half),
-        in_specs=[hbm, hbm, hbm, end, end, vmem, smem, smem, smem, smem],
+        in_specs=[hbm, hbm, hbm, vmem, smem, smem, smem, smem],
         out_specs=(vmem, vmem, vmem),
         scratch_shapes=main_scratch() + tail_scratch(),
         compiler_params=pltpu.CompilerParams(
             collective_id=1, has_side_effects=True, vmem_limit_bytes=56 * 2**20),
         name="tower",
-    )(patches.T, inner, outer_weight, inner, outer_weight, text_embed, counts, pair_ids, log_scale, logit_bias)
+    )(patches.T, inner_weight.T, outer_weight, text_embed, counts, pair_ids, log_scale, logit_bias)
     return pl.pallas_call(
         hand_over,
         out_shape=(jax.ShapeDtypeStruct((2,), F32), half, half),

time: 69.4 us -> 68.2 us (0.983)
  Pallas kernels: 67.1 us -> 66 us
    pallas_call x1, Pallas kernels: 65.8 us -> 64.7 us  [shards(): pl.pallas_call(main_kernel, out_shape=(jax.ShapeDtypeStruct((2, 128), F32...]
where the time goes in v5:
time: 68.2 us; the launch traced here: 68.1 us
  Pallas kernels  66 us (97%)
  between operations  2.09 us (3%)
    pallas_call x1, Pallas kernels, shards(): pl.pallas_call(main_kernel, out_shape=(jax.ShapeDtypeStruct((2, 128), F32...  64.7 us

profile of v5, /device:TPU:1, one launch (start us, length us, event | category | flops | bytes accessed | tf_op | source)
XLA Modules:
  0.0 68.1 jit_solution(18368441112343105438)
XLA Ops:
  1.9 64.7 %tower.1 = (f32[2,128]{1,0:T(2,128)}, f32[2,288]{1,0:T(2,128)}, f32[2,288]{1,0:T(2,128)}) custom-call(bf16[288,2048]{1,0:T(8,128)(2,1)} %bitcast.3, bf16[1076,1152]{1,0:T(8,128)(2,1)} %bitcast.2, bf16[1076,1152]{1,0:T(8,128)(2,1)} %outer_ref.1, bf16[2,288]{1,0:T(2,128)(2,1)} %text_ref.1, s32[2]{0:T(128)} %counts_ref.1, s32[2]{0:T(128)} %pair_ref.1, ...), custom_call_target="tpu_custom_call" | custom-call | tf_op jit(solution)/shard_map/tower/pallas_call | solution.py:513
  66.6 1.3 %hand_over.1 = (f32[2]{0:T(128)}, f32[2,288]{1,0:T(2,128)}, f32[2,288]{1,0:T(2,128)}) custom-call(f32[2,128]{1,0:T(2,128)} %get-tuple-element.6.loss_ref, f32[2,288]{1,0:T(2,128)} %get-tuple-element.7.emb_ref, f32[2,288]{1,0:T(2,128)} %get-tuple-element.8.txt_ref), custom_call_target="tpu_custom_call" | custom-call | tf_op jit(solution)/shard_map/hand_over/pallas_call | solution.py:523

commit v6 on v5

--- a/solution.py
+++ b/solution.py
@@ -232,11 +232,11 @@
 MAIN = 1024
 TAIL = 64
 UNITS = 1076
-WINDOW = 6
+WINDOW = 5
 STAGES = 9
-HI = [(1, 0), (2, 0), (2, 1), (0, 0), (0, 1), (3, 0), (3, 1), (4, 1), (5, 1), (6, 0), (6, 1), (8, 0)]
-LO = [('P', 0), ('P', 1), (1, 1), ('P', 2), (4, 0), ('P', 3), (5, 0), (7, 0), (7, 1), (8, 1)]
-ORDER = [('F', 1, 0), ('F', 2, 0), ('N', 0), ('F', 2, 1), ('e', 0, 0), ('F', 0, 0), ('e', 0, 1), ('F', 0, 1), ('N', 1), ('m', 0), ('F', 3, 0), ('F', 1, 1), ('e', 1, 0), ('e', 1, 1), ('F', 3, 1), ('m', 1), ('H', 0, 0), ('H', 0, 2), ('F', 4, 1), ('N', 2), ('F', 4, 0), ('F', 5, 1), ('H', 0, 1), ('F', 6, 0), ('H', 0, 3), ('F', 6, 1), ('N', 3), ('H', 0, 4), ('F', 5, 0), ('F', 8, 0), ('E', 1, 0), ('E', 1, 1), ('E', 1, 2), ('F', 7, 0), ('E', 1, 3), ('M', 1, 0), ('F', 7, 1), ('M', 1, 1), ('H', 1, 0), ('H', 1, 1), ('F', 8, 1), ('H', 1, 2), ('H', 1, 3), ('H', 1, 4), ('A', 0, 0), ('A', 0, 1), ('A', 1, 0), ('A', 1, 1), ('B', 0), ('B', 1)]
+HI = [(1, 0), (1, 1), (2, 0), (2, 1), (0, 0), (0, 1), (3, 0), (4, 1), (5, 1), (6, 0), (6, 1), (7, 1), (8, 0), (8, 1)]
+LO = [(3, 1), ('P', 0), ('P', 1), (4, 0), ('P', 2), ('P', 3), (5, 0), (7, 0)]
+ORDER = [('F', 1, 0), ('F', 3, 1), ('F', 1, 1), ('F', 2, 0), ('N', 0), ('F', 2, 1), ('e', 0, 0), ('F', 0, 0), ('e', 0, 1), ('F', 0, 1), ('N', 1), ('m', 0), ('F', 3, 0), ('F', 4, 0), ('e', 1, 0), ('e', 1, 1), ('F', 4, 1), ('m', 1), ('H', 0, 0), ('H', 0, 1), ('F', 5, 1), ('N', 2), ('H', 0, 2), ('H', 0, 3), ('F', 6, 0), ('F', 6, 1), ('N', 3), ('H', 0, 4), ('F', 5, 0), ('F', 7, 1), ('E', 1, 0), ('E', 1, 1), ('E', 1, 2), ('F', 7, 0), ('F', 8, 0), ('E', 1, 3), ('M', 1, 0), ('F', 8, 1), ('M', 1, 1), ('H', 1, 0), ('H', 1, 1), ('H', 1, 2), ('H', 1, 3), ('H', 1, 4), ('A', 0, 0), ('A', 0, 1), ('A', 1, 0), ('A', 1, 1), ('B', 0), ('B', 1)]
 
 
 def main_peers():
@@ -261,9 +261,9 @@
 
 
 def main_kernel(
-    patch_ref, inner_ref, outer_ref, text_ref, counts_ref, pair_ref, scale_ref, bias_ref,
+    patch_ref, inner_ref, outer_ref, text_hbm, counts_hbm, pair_hbm, scale_hbm, bias_hbm,
     loss_ref, emb_ref, txt_ref,
-    w1_own, w2_own, tails, w1_oth, w2_oth, xin, xres, xn, acc, hid, part_out, part_in,
+    text_ref, counts_ref, pair_ref, scale_ref, bias_ref, small_sem, w1_own, w2_own, tails, w1_oth, w2_oth, xin, xres, xn, acc, hid, part_out, part_in,
     load_sem, own_sem, patch_send, patch_recv, norm_send, norm_recv, y_send, y_recv,
     side_send, side_recv, part_send, part_recv, heard, *tail_refs,
 ):
@@ -275,6 +275,9 @@
     barrier = pltpu.get_barrier_semaphore()
     for peer in peers.values():
         pl.semaphore_signal(barrier, inc=1, device_id=peer, device_id_type=MESH)
+    smalls = [pltpu.make_async_copy(src, dst, small_sem.at[n]) for n, (src, dst) in enumerate((
+        (text_hbm, text_ref), (counts_hbm, counts_ref), (pair_hbm, pair_ref), (scale_hbm, scale_ref),
+        (bias_hbm, bias_ref)))]
     loads = [
         pltpu.make_async_copy(inner_ref, w1_own, load_sem.at[0]),
         pltpu.make_async_copy(outer_ref, w2_own, load_sem.at[1]),
@@ -283,9 +286,10 @@
         pltpu.make_async_copy(
             patch_ref.at[:, pl.ds(pl.multiple_of(ROWS * mp + 128 * rb, 128), 128)], xin.at[rb, mp], own_sem.at[rb])
         for rb in range(4)]
-    for copy in mine + loads:
+    for copy in smalls + mine + loads:
         copy.start()
     tail = Tail(text_ref, counts_ref, pair_ref, scale_ref, bias_ref, loss_ref, emb_ref, txt_ref, *tail_refs)
+    smalls[0].wait()
     tail.begin()
     pl.semaphore_wait(barrier, len(peers))
 
@@ -419,6 +423,8 @@
     for _ in range(2):
         issue("hi")
         issue("lo")
+    for copy in smalls[1:]:
+        copy.wait()
     kept = inner_ref.shape[0] - MAIN
     for k, (own, oth) in enumerate(((w1_own, w1_oth), (w2_own, w2_oth))):
         loads[k].wait()
@@ -486,6 +492,8 @@
 def main_scratch():
     dma = pltpu.SemaphoreType.DMA
     return [
+        pltpu.VMEM((2, DL), BF16), pltpu.SMEM((2,), jnp.int32), pltpu.SMEM((2,), jnp.int32), pltpu.SMEM((1,), F32),
+        pltpu.SMEM((1,), F32), dma((5,)),
         pltpu.VMEM((UNITS, D), BF16), pltpu.VMEM((UNITS, D), BF16), pltpu.VMEM((2, TAIL, D), BF16),
         pltpu.VMEM((D, D), BF16), pltpu.VMEM((D, D), BF16),
         pltpu.VMEM((4, 4, DL, 128), BF16), pltpu.VMEM((4, 128, D), BF16),
@@ -513,7 +521,7 @@
     found = pl.pallas_call(
         main_kernel,
         out_shape=(jax.ShapeDtypeStruct((2, 128), F32), half, half),
-        in_specs=[hbm, hbm, hbm, vmem, smem, smem, smem, smem],
+        in_specs=[hbm] * 8,
         out_specs=(vmem, vmem, vmem),
         scratch_shapes=main_scratch() + tail_scratch(),
         compiler_params=pltpu.CompilerParams(

time: 68.2 us -> 66.8 us (0.979)
  Pallas kernels: 66 us -> 64.6 us
    pallas_call x1, Pallas kernels: 64.7 us -> 63.3 us  [shards(): pl.pallas_call(main_kernel, out_shape=(jax.ShapeDtypeStruct((2, 128), F32...]
where the time goes in v6:
time: 66.8 us; the launch traced here: 66.7 us
  Pallas kernels  64.6 us (97%)
  between operations  2.09 us (3%)
    pallas_call x1, Pallas kernels, shards(): pl.pallas_call(main_kernel, out_shape=(jax.ShapeDtypeStruct((2, 128), F32...  63.3 us

profile of v6, /device:TPU:1, one launch (start us, length us, event | category | flops | bytes accessed | tf_op | source)
XLA Modules:
  0.0 66.7 jit_solution(11261517700342776076)
XLA Ops:
  1.9 63.3 %tower.1 = (f32[2,128]{1,0:T(2,128)}, f32[2,288]{1,0:T(2,128)}, f32[2,288]{1,0:T(2,128)}) custom-call(bf16[288,2048]{1,0:T(8,128)(2,1)} %bitcast.3, bf16[1076,1152]{1,0:T(8,128)(2,1)} %bitcast.2, bf16[1076,1152]{1,0:T(8,128)(2,1)} %outer_ref.1, bf16[2,288]{1,0:T(2,128)(2,1)} %text_hbm.1, s32[2]{0:T(128)} %counts_hbm.1, s32[2]{0:T(128)} %pair_hbm.1, ...), custom_call_target="tpu_custom_call" | custom-call | tf_op jit(solution)/shard_map/tower/pallas_call | solution.py:521
  65.2 1.3 %hand_over.1 = (f32[2]{0:T(128)}, f32[2,288]{1,0:T(2,128)}, f32[2,288]{1,0:T(2,128)}) custom-call(f32[2,128]{1,0:T(2,128)} %get-tuple-element.6.loss_ref, f32[2,288]{1,0:T(2,128)} %get-tuple-element.7.emb_ref, f32[2,288]{1,0:T(2,128)} %get-tuple-element.8.txt_ref), custom_call_target="tpu_custom_call" | custom-call | tf_op jit(solution)/shard_map/hand_over/pallas_call | solution.py:531

commit v7 on v6

--- a/solution.py
+++ b/solution.py
@@ -289,8 +289,6 @@
     for copy in smalls + mine + loads:
         copy.start()
     tail = Tail(text_ref, counts_ref, pair_ref, scale_ref, bias_ref, loss_ref, emb_ref, txt_ref, *tail_refs)
-    smalls[0].wait()
-    tail.begin()
     pl.semaphore_wait(barrier, len(peers))
 
     def patch_copies(rb):
@@ -419,10 +417,12 @@
             part_out[rb] = acc[half, 2 * r + 1 - core].astype(BF16)
             part_copy(rb).start()
 
-    tail.greet()
     for _ in range(2):
         issue("hi")
         issue("lo")
+    smalls[0].wait()
+    tail.begin()
+    tail.greet()
     for copy in smalls[1:]:
         copy.wait()
     kept = inner_ref.shape[0] - MAIN

time: 66.8 us -> 66.8 us (level)
  no operation moved by 1% of the time
where the time goes in v7:
time: 66.8 us; the launch traced here: 66.7 us
  Pallas kernels  64.6 us (97%)
  between operations  2.09 us (3%)
    pallas_call x1, Pallas kernels, shards(): pl.pallas_call(main_kernel, out_shape=(jax.ShapeDtypeStruct((2, 128), F32...  63.3 us

profile of v7, /device:TPU:1, one launch (start us, length us, event | category | flops | bytes accessed | tf_op | source)
XLA Modules:
  0.0 66.7 jit_solution(8003817775169204958)
XLA Ops:
  1.9 63.3 %tower.1 = (f32[2,128]{1,0:T(2,128)}, f32[2,288]{1,0:T(2,128)}, f32[2,288]{1,0:T(2,128)}) custom-call(bf16[288,2048]{1,0:T(8,128)(2,1)} %bitcast.3, bf16[1076,1152]{1,0:T(8,128)(2,1)} %bitcast.2, bf16[1076,1152]{1,0:T(8,128)(2,1)} %outer_ref.1, bf16[2,288]{1,0:T(2,128)(2,1)} %text_hbm.1, s32[2]{0:T(128)} %counts_hbm.1, s32[2]{0:T(128)} %pair_hbm.1, ...), custom_call_target="tpu_custom_call" | custom-call | tf_op jit(solution)/shard_map/tower/pallas_call | solution.py:521
  65.2 1.3 %hand_over.1 = (f32[2]{0:T(128)}, f32[2,288]{1,0:T(2,128)}, f32[2,288]{1,0:T(2,128)}) custom-call(f32[2,128]{1,0:T(2,128)} %get-tuple-element.6.loss_ref, f32[2,288]{1,0:T(2,128)} %get-tuple-element.7.emb_ref, f32[2,288]{1,0:T(2,128)} %get-tuple-element.8.txt_ref), custom_call_target="tpu_custom_call" | custom-call | tf_op jit(solution)/shard_map/hand_over/pallas_call | solution.py:531
